TPU v7x, 32 devices: a whole 2x2x4 slice. The times are simulated.
32 devices in a mesh: dp: 16 (over z, x, core), tensor: 2 (over y).
Axes of the slice: x: 2, y: 2, z: 4, core: 2. Of those that a mesh axis runs over, the one named last changes fastest.
Arguments:
- tokens: bfloat16 [8192, 768], P('dp'), may hold values from -6 to 6
- query_weight: bfloat16 [2, 768, 768], P(None, None, 'tensor'), may hold values from -0.02734375 to 0.02734375
- key_weight: bfloat16 [2, 768, 768], P(None, None, 'tensor'), may hold values from -0.21875 to 0.21875
- value_weight: bfloat16 [2, 768, 768], P(None, None, 'tensor'), may hold values from -0.21875 to 0.21875
- output_weight: bfloat16 [2, 768, 768], P(None, 'tensor'), may hold values from -1.75 to 1.75
- prenorm_gain: bfloat16 [2, 768], replicated, may hold values from 0.5 to 1.5
- midnorm_gain: bfloat16 [2, 768], replicated, may hold values from 0.5 to 1.5
- bucket_bias_table: bfloat16 [2, 32, 12], P(None, None, 'tensor'), may hold values from -4 to 4
- router_weight: bfloat16 [2, 768, 3], replicated, may hold values from -0.15625 to 0.15625
- expert_up: bfloat16 [2, 3, 768, 3072], P(None, None, None, 'tensor'), may hold values from -0.21875 to 0.21875
- expert_down: bfloat16 [2, 3, 3072, 768], P(None, None, 'tensor'), may hold values from -0.3125 to 0.3125
- lengths: int32 [16, 4], P('dp'), may hold values from 0 to 512, as said below
- expert_ids: int32 [8192, 1], P('dp'), may hold values from 0 to 2
- cotangent: bfloat16 [8192, 768], P('dp'), may hold values from -6 to 6
Outputs:
- activations: bfloat16 [8192, 768], P('dp')
- input_grad: float32 [8192, 768], P('dp')
- query_weight_grad: float32 [2, 768, 768], P(None, 'dp', 'tensor')
- key_grad: float32 [2, 768, 768], P(None, 'dp', 'tensor')
- value_grad: float32 [2, 768, 768], P(None, 'dp', 'tensor')
- output_grad: float32 [2, 768, 768], P(None, 'tensor', 'dp')
- prenorm_grad: float32 [2, 768], P(None, 'dp')
- midnorm_grad: float32 [2, 768], P(None, 'dp')
- table_grad: float32 [2, 32, 12], P(None, None, 'tensor')
- router_grad: float32 [2, 768, 3], P(None, 'dp')
- expert_up_grad: float32 [2, 3, 768, 3072], P(None, None, 'dp', 'tensor')
- down_grad: float32 [2, 3, 3072, 768], P(None, None, 'tensor', 'dp')
Inputs may be any that keep to these rules, and one draw needn't show every extreme that they name: Row r gives the lengths of the 4 sequences packed from the start of block r; a row sums to 512 or less, lengths may be 0, and some row holds one sequence of 512.
All inputs are finite; a program needn't handle non-finite values.
Results may differ from a plain program's by a relative error of at most 0.022.
Values sent between devices are 32-bit elements; how exact they have to be, the bound alone decides.
A program may use at most 320 MiB of HBM per device.

v0:
```python
import jax
import jax.numpy as jnp
from jax import lax
from jax.sharding import PartitionSpec as P

POSITION_BUCKETS = 32
EXPERTS = 3
LAYERS = 2
CAP = 170


LIMITS = (12, 16, 23, 32, 46, 64, 91)
EPSILON = 1e-06
PRECISE = lax.Precision.HIGHEST


def bucket_ids(query_pos, key_pos):
    relative = key_pos[None, :] - query_pos[:, None]
    distance = jnp.abs(relative)
    beyond = 8 + sum(((distance >= limit_at).astype(jnp.int32) for limit_at in LIMITS))
    return jnp.where(distance < 8, distance, beyond) + 16 * (relative > 0).astype(jnp.int32)


def rms_norm(stream, scale_gain):
    return (
        stream * lax.rsqrt(jnp.mean(stream * stream, axis=-1, keepdims=True) + EPSILON) * scale_gain
    )


def gelu_tanh(values):
    return jax.nn.gelu(values, approximate=True)


def segments(length_row, row_count):
    ends_at = jnp.cumsum(length_row, dtype=jnp.int32)
    position = jnp.arange(row_count, dtype=jnp.int32)
    segment = jnp.sum(
        (position[:, None] >= ends_at[None, :]).astype(jnp.int32), axis=1, dtype=jnp.int32
    )
    alive_rows = position < ends_at[-1]
    return (jnp.where(alive_rows, segment, -1), alive_rows)


def slot_of(expert_pick, alive_rows):
    picked_expert = (
        (expert_pick[:, None] == jnp.arange(EXPERTS, dtype=jnp.int32)[None, :])
        & alive_rows[:, None]
    ).astype(jnp.int32)
    prior_value = jnp.cumsum(picked_expert, axis=0, dtype=jnp.int32) - picked_expert
    position = jnp.sum(prior_value * picked_expert, axis=1, dtype=jnp.int32)
    return jnp.where(alive_rows & (position < CAP), position, CAP)


def attention_scores(query_rows, key_rows, bucket_bias_table, segment, bucket_indicator):
    row_count = query_rows.shape[0]
    heads_here = bucket_bias_table.shape[1]
    pos_bias = jnp.einsum(
        "cgp,cf->fgp", bucket_indicator, bucket_bias_table, preferred_element_type=jnp.float32
    )
    query_split = query_rows.reshape(row_count, heads_here, -1)
    key_split = key_rows.reshape(row_count, heads_here, -1)
    scores = (
        jnp.einsum("qhd,khd->hqk", query_split, key_split, preferred_element_type=jnp.float32)
        + pos_bias
    )
    same_sequence = segment[:, None] == segment[None, :]
    return jnp.where(same_sequence[None], scores, -1000000000.0)


def forward_layer(
    stream, weight_set, segment, expert_pick, expert_slot_index, sources, bucket_indicator
):
    (
        query_weight,
        key_weight,
        value_weight,
        output_weight,
        prenorm_gain,
        midnorm_gain,
        bucket_bias_table,
        router_weight,
        expert_up,
        expert_down,
    ) = weight_set
    row_count, model_width = stream.shape
    heads_here = bucket_bias_table.shape[1]
    normed = rms_norm(stream, prenorm_gain.astype(jnp.float32)).astype(jnp.bfloat16)
    query_rows = jnp.dot(normed, query_weight, preferred_element_type=jnp.float32).astype(
        jnp.bfloat16
    )
    key_rows = jnp.dot(normed, key_weight, preferred_element_type=jnp.float32).astype(jnp.bfloat16)
    value_rows = jnp.dot(normed, value_weight, preferred_element_type=jnp.float32).astype(
        jnp.bfloat16
    )
    scores = attention_scores(query_rows, key_rows, bucket_bias_table, segment, bucket_indicator)
    row_peak = jnp.max(scores, axis=-1, keepdims=True)
    exponentiated = jnp.exp(scores - row_peak)
    row_total = jnp.sum(exponentiated, axis=-1, keepdims=True)
    attn_probs = (exponentiated / row_total).astype(jnp.bfloat16)
    value_split = value_rows.reshape(row_count, heads_here, -1)
    mixed_heads = (
        jnp.einsum("hqk,khd->qhd", attn_probs, value_split, preferred_element_type=jnp.float32)
        .reshape(row_count, -1)
        .astype(jnp.bfloat16)
    )
    log_total = row_peak + jnp.log(row_total)
    partial_value = jnp.dot(mixed_heads, output_weight, preferred_element_type=jnp.float32)
    attn_share = lax.psum_scatter(partial_value, "tensor", scatter_dimension=1, tiled=True)
    middle = stream + lax.all_gather(attn_share, "tensor", axis=1, tiled=True)
    second = rms_norm(middle, midnorm_gain.astype(jnp.float32)).astype(jnp.bfloat16)
    logits = jnp.dot(second, router_weight, preferred_element_type=jnp.float32)
    router_probs = jax.nn.softmax(logits, axis=-1)
    picked_expert = (expert_pick[:, None] == jnp.arange(EXPERTS, dtype=jnp.int32)[None, :]).astype(
        jnp.float32
    )
    gate_prob = jnp.sum(router_probs * picked_expert, axis=-1, keepdims=True)
    padded = jnp.concatenate([second, jnp.zeros((1, model_width), jnp.bfloat16)], axis=0)
    dispatched = padded[sources]
    hidden = jnp.einsum("ecd,edf->ecf", dispatched, expert_up, preferred_element_type=jnp.float32)
    active = gelu_tanh(hidden).astype(jnp.bfloat16)
    expert_rows = jnp.einsum(
        "ecf,efd->ecd", active, expert_down, preferred_element_type=jnp.float32
    )
    expert_rows = jnp.concatenate(
        [expert_rows, jnp.zeros((EXPERTS, 1, model_width), jnp.float32)], axis=1
    )
    expert_share = lax.psum_scatter(
        expert_rows[expert_pick, expert_slot_index], "tensor", scatter_dimension=1, tiled=True
    )
    combined = lax.all_gather(expert_share, "tensor", axis=1, tiled=True)
    saved_state = (
        stream,
        normed,
        query_rows,
        key_rows,
        value_rows,
        mixed_heads,
        log_total,
        middle,
        second,
        router_probs,
        gate_prob,
        dispatched,
        hidden,
        active,
        combined,
    )
    return (saved_state, middle + gate_prob * combined)


def layer_backward_pass(
    upstream,
    saved_state,
    weight_set,
    segment,
    expert_pick,
    expert_slot_index,
    sources,
    bucket_indicator,
):
    (
        query_weight,
        key_weight,
        value_weight,
        output_weight,
        prenorm_gain,
        midnorm_gain,
        bucket_bias_table,
        router_weight,
        expert_up,
        expert_down,
    ) = weight_set
    (
        stream,
        normed,
        query_rows,
        key_rows,
        value_rows,
        mixed_heads,
        log_total,
        middle,
        second,
        router_probs,
        gate_prob,
        dispatched,
        hidden,
        active,
        combined,
    ) = saved_state
    row_count, model_width = stream.shape
    heads_here = bucket_bias_table.shape[1]
    picked_expert = (expert_pick[:, None] == jnp.arange(EXPERTS, dtype=jnp.int32)[None, :]).astype(
        jnp.float32
    )
    combined_grad = (gate_prob * upstream).astype(jnp.bfloat16)
    gate_grad = jnp.sum(upstream * combined, axis=-1, keepdims=True)
    logit_grad = gate_grad * gate_prob * (picked_expert - router_probs)
    router_term = jnp.dot(second.astype(jnp.float32).T, logit_grad, precision=PRECISE)
    second_grad = jnp.dot(logit_grad, router_weight.astype(jnp.float32).T, precision=PRECISE)
    padded = jnp.concatenate([combined_grad, jnp.zeros((1, model_width), jnp.bfloat16)], axis=0)
    slot_grad = padded[sources]
    down_term = jnp.einsum("ecf,ecd->efd", active, slot_grad, preferred_element_type=jnp.float32)
    active_grad = jnp.einsum(
        "ecd,efd->ecf", slot_grad, expert_down, preferred_element_type=jnp.float32
    )
    hidden_grad = jax.vjp(gelu_tanh, hidden)[1](active_grad)[0].astype(jnp.bfloat16)
    up_term = jnp.einsum(
        "ecd,ecf->edf", dispatched, hidden_grad, preferred_element_type=jnp.float32
    )
    dispatch_grad = jnp.einsum(
        "ecf,edf->ecd", hidden_grad, expert_up, preferred_element_type=jnp.float32
    )
    dispatch_grad = jnp.concatenate(
        [dispatch_grad, jnp.zeros((EXPERTS, 1, model_width), jnp.float32)], axis=1
    )
    back_share = lax.psum_scatter(
        dispatch_grad[expert_pick, expert_slot_index], "tensor", scatter_dimension=1, tiled=True
    )
    second_grad = second_grad + lax.all_gather(back_share, "tensor", axis=1, tiled=True)
    middle_grad, midnorm_term = jax.vjp(rms_norm, middle, midnorm_gain.astype(jnp.float32))[1](
        second_grad
    )
    middle_grad = upstream + middle_grad
    attn_grad = middle_grad.astype(jnp.bfloat16)
    output_term = jnp.einsum(
        "tf,td->fd", mixed_heads, attn_grad, preferred_element_type=jnp.float32
    )
    mixed_grad = jnp.einsum(
        "td,fd->tf", attn_grad, output_weight, preferred_element_type=jnp.float32
    ).astype(jnp.bfloat16)
    scores = attention_scores(query_rows, key_rows, bucket_bias_table, segment, bucket_indicator)
    attn_probs = jnp.exp(scores - log_total)
    probs_low = attn_probs.astype(jnp.bfloat16)
    query_split = query_rows.reshape(row_count, heads_here, -1)
    key_split = key_rows.reshape(row_count, heads_here, -1)
    value_split = value_rows.reshape(row_count, heads_here, -1)
    mixed_split = mixed_grad.reshape(row_count, heads_here, -1)
    probs_grad = jnp.einsum(
        "qhd,khd->hqk", mixed_split, value_split, preferred_element_type=jnp.float32
    )
    center = jnp.sum(attn_probs * probs_grad, axis=-1, keepdims=True)
    score_gradient = (attn_probs * (probs_grad - center)).astype(jnp.bfloat16)
    value_back = jnp.einsum(
        "hqk,qhd->khd", probs_low, mixed_split, preferred_element_type=jnp.float32
    )
    key_back = jnp.einsum(
        "hqk,qhd->khd", score_gradient, query_split, preferred_element_type=jnp.float32
    )
    query_back = jnp.einsum(
        "hqk,khd->qhd", score_gradient, key_split, preferred_element_type=jnp.float32
    )
    table_term = jnp.einsum(
        "esm,psm->pe", score_gradient, bucket_indicator, preferred_element_type=jnp.float32
    )
    query_back = query_back.reshape(row_count, -1).astype(jnp.bfloat16)
    key_back = key_back.reshape(row_count, -1).astype(jnp.bfloat16)
    value_back = value_back.reshape(row_count, -1).astype(jnp.bfloat16)
    query_term = jnp.einsum("td,tf->df", normed, query_back, preferred_element_type=jnp.float32)
    key_term = jnp.einsum("td,tf->df", normed, key_back, preferred_element_type=jnp.float32)
    value_term = jnp.einsum("td,tf->df", normed, value_back, preferred_element_type=jnp.float32)
    normed_part = (
        jnp.einsum("tf,df->td", query_back, query_weight, preferred_element_type=jnp.float32)
        + jnp.einsum("tf,df->td", key_back, key_weight, preferred_element_type=jnp.float32)
        + jnp.einsum("tf,df->td", value_back, value_weight, preferred_element_type=jnp.float32)
    )
    normed_share = lax.psum_scatter(normed_part, "tensor", scatter_dimension=1, tiled=True)
    normed_grad = lax.all_gather(normed_share, "tensor", axis=1, tiled=True)
    stream_grad, prenorm_term = jax.vjp(rms_norm, stream, prenorm_gain.astype(jnp.float32))[1](
        normed_grad
    )
    term_set = (
        query_term,
        key_term,
        value_term,
        output_term,
        prenorm_term,
        midnorm_term,
        table_term,
        router_term,
        up_term,
        down_term,
    )
    return (middle_grad + stream_grad, term_set)


def on_device(
    tokens,
    query_weight,
    key_weight,
    value_weight,
    output_weight,
    prenorm_gain,
    midnorm_gain,
    bucket_bias_table,
    router_weight,
    expert_up,
    expert_down,
    lengths,
    expert_ids,
    cotangent,
):
    row_count = tokens.shape[0]
    segment, alive_rows = segments(lengths[0], row_count)
    expert_pick = expert_ids[:, 0]
    expert_slot_index = slot_of(expert_pick, alive_rows)
    sources = (
        jnp.full((EXPERTS, CAP + 1), row_count, jnp.int32)
        .at[expert_pick, expert_slot_index]
        .set(jnp.arange(row_count, dtype=jnp.int32))[:, :CAP]
    )
    position = jnp.arange(row_count, dtype=jnp.int32)
    bucket_map = bucket_ids(position, position)
    bucket_indicator = (
        bucket_map[None] == jnp.arange(POSITION_BUCKETS, dtype=jnp.int32)[:, None, None]
    ).astype(jnp.bfloat16)
    weight_all = (
        query_weight,
        key_weight,
        value_weight,
        output_weight,
        prenorm_gain,
        midnorm_gain,
        bucket_bias_table,
        router_weight,
        expert_up,
        expert_down,
    )
    stream = tokens.astype(jnp.float32)
    saved_list = []
    for layer_index in range(LAYERS):
        weight_set = tuple((weight_arr[layer_index] for weight_arr in weight_all))
        saved_state, stream = forward_layer(
            stream, weight_set, segment, expert_pick, expert_slot_index, sources, bucket_indicator
        )
        saved_list.append(saved_state)
    upstream = cotangent.astype(jnp.float32) * alive_rows[:, None].astype(jnp.float32)
    layer_terms = [None] * LAYERS
    for layer_index in reversed(range(LAYERS)):
        weight_set = tuple((weight_arr[layer_index] for weight_arr in weight_all))
        upstream, term_set = layer_backward_pass(
            upstream,
            saved_list[layer_index],
            weight_set,
            segment,
            expert_pick,
            expert_slot_index,
            sources,
            bucket_indicator,
        )
        layer_terms[layer_index] = term_set
    (
        query_weight_grad,
        key_grad,
        value_grad,
        output_grad,
        prenorm_grad,
        midnorm_grad,
        table_grad,
        router_grad,
        expert_up_grad,
        down_grad,
    ) = tuple(
        (
            jnp.stack([layer_terms[layer_index][member] for layer_index in range(LAYERS)])
            for member in range(10)
        )
    )
    (
        query_weight_grad,
        key_grad,
        value_grad,
        output_grad,
        prenorm_grad,
        midnorm_grad,
        router_grad,
        expert_up_grad,
        down_grad,
    ) = (
        lax.psum_scatter(query_weight_grad, "dp", scatter_dimension=1, tiled=True),
        lax.psum_scatter(key_grad, "dp", scatter_dimension=1, tiled=True),
        lax.psum_scatter(value_grad, "dp", scatter_dimension=1, tiled=True),
        lax.psum_scatter(output_grad, "dp", scatter_dimension=2, tiled=True),
        lax.psum_scatter(prenorm_grad, "dp", scatter_dimension=1, tiled=True),
        lax.psum_scatter(midnorm_grad, "dp", scatter_dimension=1, tiled=True),
        lax.psum_scatter(router_grad, "dp", scatter_dimension=1, tiled=True),
        lax.psum_scatter(expert_up_grad, "dp", scatter_dimension=2, tiled=True),
        lax.psum_scatter(down_grad, "dp", scatter_dimension=3, tiled=True),
    )
    table_grad = lax.psum(table_grad, "dp")
    return (
        stream.astype(jnp.bfloat16),
        upstream,
        query_weight_grad,
        key_grad,
        value_grad,
        output_grad,
        prenorm_grad,
        midnorm_grad,
        table_grad,
        router_grad,
        expert_up_grad,
        down_grad,
    )


def solution(mesh):
    return jax.shard_map(
        on_device,
        mesh=mesh,
        in_specs=(
            P("dp", None),
            P(None, None, "tensor"),
            P(None, None, "tensor"),
            P(None, None, "tensor"),
            P(None, "tensor", None),
            P(),
            P(),
            P(None, None, "tensor"),
            P(),
            P(None, None, None, "tensor"),
            P(None, None, "tensor", None),
            P("dp", None),
            P("dp", None),
            P("dp", None),
        ),
        out_specs=(
            P("dp", None),
            P("dp", None),
            P(None, "dp", "tensor"),
            P(None, "dp", "tensor"),
            P(None, "dp", "tensor"),
            P(None, "tensor", "dp"),
            P(None, "dp"),
            P(None, "dp"),
            P(None, None, "tensor"),
            P(None, "dp", None),
            P(None, None, "dp", "tensor"),
            P(None, None, "tensor", "dp"),
        ),
        check_vma=False,
    )
```

profile of v0, /device:TPU:0, one launch (start us, length us, event | category | flops | bytes accessed | tf_op | source)
XLA Modules:
  0.0 1846.7 jit_solution(13377258817634745640)
XLA Ops:
  30.9 28.9 %reduce-scatter.22.cloned.1.call-done = f32[512,384]{1,0:T(8,128)} async-done(((f32[512,768]{1,0:T(8,128)}), f32[512,384]{1,0:T(8,128)}) %reduce-scatter.22.cloned.1.call-update) | async-done | bytes 786448 | tf_op jit(solution)/shard_map/reduce_scatter | solution.py:108
  63.5 24.7 %scatter_fusion = s32[3,171]{1,0:T(4,128)S(1)} fusion(s32[3,171]{1,0:T(4,128)S(1)} %broadcast_in_dim.44, s32[512]{0:T(512)S(1)} %bitcast.266, s32[512]{0:T(512)S(1)} %iota.68), kind=kCustom, calls=%fused_computation.8 | custom fusion | bytes 10240 | tf_op jit(solution)/shard_map/scatter | solution.py:309
  114.1 26.2 %reduce-scatter.24.cloned.1.call-done = f32[512,384]{1,0:T(8,128)} async-done(((f32[512,768]{1,0:T(8,128)}), f32[512,384]{1,0:T(8,128)}) %reduce-scatter.24.cloned.1.call-update) | async-done | bytes 786448 | tf_op jit(solution)/shard_map/reduce_scatter | solution.py:127
  148.9 20.0 %all-gather.11.cloned.1.call-done = f32[512,768]{1,0:T(8,128)} async-done(((f32[512,384]{1,0:T(8,128)}), f32[512,768]{1,0:T(8,128)}) %all-gather.11.cloned.1.call-update) | async-done | bytes 1572880 | tf_op jit(solution)/shard_map/all_gather | solution.py:130
  186.0 26.2 %reduce-scatter.26.cloned.1.call-done = f32[512,384]{1,0:T(8,128)} async-done(((f32[512,768]{1,0:T(8,128)}), f32[512,384]{1,0:T(8,128)}) %reduce-scatter.26.cloned.1.call-update) | async-done | bytes 786448 | tf_op jit(solution)/shard_map/reduce_scatter | solution.py:108
  212.7 28.2 %all-gather.13.cloned.1.call-done = f32[512,768]{1,0:T(8,128)} async-done(((f32[512,384]{1,0:T(8,128)}), f32[512,768]{1,0:T(8,128)}) %all-gather.13.cloned.1.call-update) | async-done | bytes 1572880 | tf_op jit(solution)/shard_map/all_gather | solution.py:109
  265.4 26.2 %reduce-scatter.28.cloned.1.call-done = f32[512,384]{1,0:T(8,128)} async-done(((f32[512,768]{1,0:T(8,128)}), f32[512,384]{1,0:T(8,128)}) %reduce-scatter.28.cloned.1.call-update) | async-done | bytes 786448 | tf_op jit(solution)/shard_map/reduce_scatter | solution.py:127
  292.9 27.5 %all-gather.15.cloned.1.call-done = f32[512,768]{1,0:T(8,128)} async-done(((f32[512,384]{1,0:T(8,128)}), f32[512,768]{1,0:T(8,128)}) %all-gather.15.cloned.1.call-update) | async-done | bytes 1572880 | tf_op jit(solution)/shard_map/all_gather | solution.py:130
  346.5 26.2 %reduce-scatter.30.cloned.1.call-done = f32[512,384]{1,0:T(8,128)} async-done(((f32[512,768]{1,0:T(8,128)}), f32[512,384]{1,0:T(8,128)}) %reduce-scatter.30.cloned.1.call-update) | async-done | bytes 786448 | tf_op jit(solution)/shard_map/reduce_scatter | solution.py:216
  373.0 28.4 %all-gather.17.cloned.1.call-done = f32[512,768]{1,0:T(8,128)} async-done(((f32[512,384]{1,0:T(8,128)}), f32[512,768]{1,0:T(8,128)}) %all-gather.17.cloned.1.call-update) | async-done | bytes 1572880 | tf_op jit(solution)/shard_map/all_gather | solution.py:219
  419.3 26.2 %reduce-scatter.32.cloned.1.call-done = f32[512,384]{1,0:T(8,128)} async-done(((f32[512,768]{1,0:T(8,128)}), f32[512,384]{1,0:T(8,128)}) %reduce-scatter.32.cloned.1.call-update) | async-done | bytes 786448 | tf_op jit(solution)/shard_map/reduce_scatter | solution.py:266
  445.9 28.3 %all-gather.19.cloned.1.call-done = f32[512,768]{1,0:T(8,128)} async-done(((f32[512,384]{1,0:T(8,128)}), f32[512,768]{1,0:T(8,128)}) %all-gather.19.cloned.1.call-update) | async-done | bytes 1572880 | tf_op jit(solution)/shard_map/all_gather | solution.py:267
  504.2 26.2 %reduce-scatter.34.cloned.1.call-done = f32[512,384]{1,0:T(8,128)} async-done(((f32[512,768]{1,0:T(8,128)}), f32[512,384]{1,0:T(8,128)}) %reduce-scatter.34.cloned.1.call-update) | async-done | bytes 786448 | tf_op jit(solution)/shard_map/reduce_scatter | solution.py:216
  531.0 28.2 %all-gather.21.cloned.1.call-done = f32[512,768]{1,0:T(8,128)} async-done(((f32[512,384]{1,0:T(8,128)}), f32[512,768]{1,0:T(8,128)}) %all-gather.21.cloned.1.call-update) | async-done | bytes 1572880 | tf_op jit(solution)/shard_map/all_gather | solution.py:219
  604.2 21.4 %pad_maximum_fusion.1 = f32[2,3,1536,768]{3,2,1,0:T(8,128)} fusion(f32[1,3,1536,768]{3,2,1,0:T(8,128)} %convolution_bitcast_fusion, f32[1,3,1536,768]{3,2,1,0:T(8,128)} %convolution_bitcast_fusion.1), kind=kLoop, calls=%fused_computation.15 | loop fusion | flops 7077888 | bytes 56623104 | tf_op jit(solution)/shard_map/stack | solution.py:364
  625.6 41.9 %copy.101 = f32[2,3,1536,768]{2,0,1,3:T(2,128)} copy(f32[2,3,1536,768]{3,2,1,0:T(8,128)} %pad_maximum_fusion.1) | data formatting | bytes 56623104 | tf_op jit(solution)/shard_map/stack | solution.py:364
  732.8 31.4 %psum.7 = f32[2,32,6]{1,2,0:T(8,128)S(1)} all-reduce(f32[2,32,6]{1,2,0:T(8,128)S(1)} %pad_maximum_fusion.7), channel_id=1, replica_groups=mesh['dp'=16,'tensor'=2] {'dp'}, use_global_device_ids=true, to_apply=%region_46.47 | all-reduce | flops 384 | bytes 3072 | tf_op jit(solution)/shard_map/psum | solution.py:389
  764.8 16.8 reduce-scatter.48.cloned.1.call-done
  786.0 53.8 %reduce-scatter.46.cloned.1.call-done = f32[48,2]{1,0:T(8,128)} async-done(((f32[768,2]{1,0:T(8,128)}), f32[48,2]{1,0:T(8,128)}) %reduce-scatter.46.cloned.1.call-update) | async-done | bytes 400
  841.1 524.3 %all-reduce.13.cloned.1.call-done = (f32[2,384,768]{1,0,2:T(2,128)}, f32[2,3,1536,768]{2,0,1,3:T(2,128)}) async-done(((f32[2,384,768]{1,0,2:T(2,128)}, f32[2,3,1536,768]{2,0,1,3:T(2,128)}), (f32[2,384,768]{1,0,2:T(2,128)}, f32[2,3,1536,768]{2,0,1,3:T(2,128)})) %all-reduce.13.cloned.1.call-update) | async-done | bytes 30670864
  1370.7 62.2 %reduce-scatter.42.cloned.1.call-done = f32[2,48,384]{2,1,0:T(8,128)} async-done(((f32[2,768,384]{2,1,0:T(8,128)}), f32[2,48,384]{2,1,0:T(8,128)}) %reduce-scatter.42.cloned.1.call-update) | async-done | bytes 147472 | tf_op jit(solution)/shard_map/reduce_scatter | solution.py:381
  1432.8 66.8 %reduce-scatter.40.cloned.1.call-done = f32[2,48,384]{2,1,0:T(8,128)} async-done(((f32[2,768,384]{2,1,0:T(8,128)}), f32[2,48,384]{2,1,0:T(8,128)}) %reduce-scatter.40.cloned.1.call-update) | async-done | bytes 147472 | tf_op jit(solution)/shard_map/reduce_scatter | solution.py:380
  1499.6 66.3 %reduce-scatter.38.cloned.1.call-done = f32[2,48,384]{2,1,0:T(8,128)} async-done(((f32[2,768,384]{2,1,0:T(8,128)}), f32[2,48,384]{2,1,0:T(8,128)}) %reduce-scatter.38.cloned.1.call-update) | async-done | bytes 147472 | tf_op jit(solution)/shard_map/reduce_scatter | solution.py:379
  1566.0 273.6 %reduce-scatter.44.cloned.1.call-done = f32[2,3,48,1536]{3,2,1,0:T(8,128)} async-done(((f32[2,3,768,1536]{3,2,1,0:T(8,128)}), f32[2,3,48,1536]{3,2,1,0:T(8,128)}) %reduce-scatter.44.cloned.1.call-update) | async-done | bytes 1769488 | tf_op jit(solution)/shard_map/reduce_scatter | solution.py:386
  (426 shorter events, 299.9 us)
Async XLA Ops:
  7.2 52.5 %reduce-scatter.22.cloned.1.call-start = ((), (), s32[]{:S(2)}) async-start(), calls=%async_computation.15 | async-start | bytes 2359296 | tf_op jit(solution)/shard_map/reduce_scatter | solution.py:108
  30.8 57.8 %all-gather.9.cloned.1.call-start = ((), (), s32[]{:S(2)}) async-start(), calls=%async_computation.16 | async-start | bytes 2359296 | tf_op jit(solution)/shard_map/all_gather | solution.py:109
  59.8 80.5 %reduce-scatter.24.cloned.1.call-start = ((), (), s32[]{:S(2)}) async-start(), calls=%async_computation.17 | async-start | bytes 2359296 | tf_op jit(solution)/shard_map/reduce_scatter | solution.py:127
  114.0 54.9 %all-gather.11.cloned.1.call-start = ((), (), s32[]{:S(2)}) async-start(), calls=%async_computation.18 | async-start | bytes 2359296 | tf_op jit(solution)/shard_map/all_gather | solution.py:130
  140.3 71.9 %reduce-scatter.26.cloned.1.call-start = ((), (), s32[]{:S(2)}) async-start(), calls=%async_computation.19 | async-start | bytes 2359296 | tf_op jit(solution)/shard_map/reduce_scatter | solution.py:108
  185.9 55.0 %all-gather.13.cloned.1.call-start = ((), (), s32[]{:S(2)}) async-start(), calls=%async_computation.20 | async-start | bytes 2359296 | tf_op jit(solution)/shard_map/all_gather | solution.py:109
  212.2 79.4 %reduce-scatter.28.cloned.1.call-start = ((), (), s32[]{:S(2)}) async-start(), calls=%async_computation.21 | async-start | bytes 2359296 | tf_op jit(solution)/shard_map/reduce_scatter | solution.py:127
  265.4 55.0 %all-gather.15.cloned.1.call-start = ((), (), s32[]{:S(2)}) async-start(), calls=%async_computation.22 | async-start | bytes 2359296 | tf_op jit(solution)/shard_map/all_gather | solution.py:130
  291.6 81.0 %reduce-scatter.30.cloned.1.call-start = ((), (), s32[]{:S(2)}) async-start(), calls=%async_computation.23 | async-start | bytes 2359296 | tf_op jit(solution)/shard_map/reduce_scatter | solution.py:216
  346.4 55.0 %all-gather.17.cloned.1.call-start = ((), (), s32[]{:S(2)}) async-start(), calls=%async_computation.24 | async-start | bytes 2359296 | tf_op jit(solution)/shard_map/all_gather | solution.py:219
  372.7 72.8 %reduce-scatter.32.cloned.1.call-start = ((), (), s32[]{:S(2)}) async-start(), calls=%async_computation.25 | async-start | bytes 2359296 | tf_op jit(solution)/shard_map/reduce_scatter | solution.py:266
  419.3 54.9 %all-gather.19.cloned.1.call-start = ((), (), s32[]{:S(2)}) async-start(), calls=%async_computation.26 | async-start | bytes 2359296 | tf_op jit(solution)/shard_map/all_gather | solution.py:267
  445.6 84.9 %reduce-scatter.34.cloned.1.call-start = ((), (), s32[]{:S(2)}) async-start(), calls=%async_computation.27 | async-start | bytes 2359296 | tf_op jit(solution)/shard_map/reduce_scatter | solution.py:216
  504.2 55.0 %all-gather.21.cloned.1.call-start = ((), (), s32[]{:S(2)}) async-start(), calls=%async_computation.28 | async-start | bytes 2359296 | tf_op jit(solution)/shard_map/all_gather | solution.py:219
  530.4 71.5 %reduce-scatter.36.cloned.1.call-start = ((), (), s32[]{:S(2)}) async-start(), calls=%async_computation.29 | async-start | bytes 2359296 | tf_op jit(solution)/shard_map/reduce_scatter | solution.py:266
  575.7 94.5 %all-gather.23.cloned.1.call-start = ((), (), s32[]{:S(2)}) async-start(), calls=%async_computation.30 | async-start | bytes 2359296 | tf_op jit(solution)/shard_map/all_gather | solution.py:267
  602.0 121.2 %reduce-scatter.50.cloned.1.call-start = ((), (), s32[]{:S(2)}) async-start(), calls=%async_computation.37 | async-start | bytes 417792
  667.6 114.0 %reduce-scatter.48.cloned.1.call-start = ((), (), s32[]{:S(2)}) async-start(), calls=%async_computation.36 | async-start | bytes 417792
  670.2 169.5 %reduce-scatter.46.cloned.1.call-start = ((), (), s32[]{:S(2)}) async-start(), calls=%async_computation.35 | async-start | bytes 417792
  673.3 692.2 %all-reduce.13.cloned.1.call-start = ((), (), s32[]{:S(2)}) async-start(), calls=%async_computation.38 | async-start | bytes 61341696
  682.0 750.9 %reduce-scatter.42.cloned.1.call-start = ((), (), s32[]{:S(2)}) async-start(), calls=%async_computation.33 | async-start | bytes 2506752 | tf_op jit(solution)/shard_map/reduce_scatter | solution.py:381
  686.6 813.1 %reduce-scatter.40.cloned.1.call-start = ((), (), s32[]{:S(2)}) async-start(), calls=%async_computation.32 | async-start | bytes 2506752 | tf_op jit(solution)/shard_map/reduce_scatter | solution.py:380
  690.9 875.1 %reduce-scatter.38.cloned.1.call-start = ((), (), s32[]{:S(2)}) async-start(), calls=%async_computation.31 | async-start | bytes 2506752 | tf_op jit(solution)/shard_map/reduce_scatter | solution.py:379
  695.2 1144.3 %reduce-scatter.44.cloned.1.call-start = ((), (), s32[]{:S(2)}) async-start(), calls=%async_computation.34 | async-start | bytes 30081024 | tf_op jit(solution)/shard_map/reduce_scatter | solution.py:386
  (103 other events, 894.0 us)
Sparse Core Ops, SparseCore 0:
  30.9 28.7 reduce-scatter.21
  61.4 27.2 all-gather.8
  114.1 26.0 reduce-scatter.23
  141.7 27.1 all-gather.10
  186.1 26.0 reduce-scatter.25
  213.7 27.1 all-gather.12
  265.5 26.0 reduce-scatter.27
  293.2 27.2 all-gather.14
  346.6 26.0 reduce-scatter.29
  374.2 27.2 all-gather.16
  419.4 26.0 reduce-scatter.31
  446.9 27.1 all-gather.18
  504.3 26.0 reduce-scatter.33
  531.9 27.1 all-gather.20
  575.9 26.0 reduce-scatter.35
  603.4 27.2 all-gather.22
  667.7 55.5 reduce-scatter.49
  727.0 54.6 reduce-scatter.47
  785.1 54.5 reduce-scatter.45
  844.6 520.8 all-reduce.12
  1369.8 62.9 reduce-scatter.41
  1437.7 61.9 reduce-scatter.39
  1504.0 61.9 reduce-scatter.37
  1571.2 268.3 reduce-scatter.43
where the time goes:
time: 1860 us; the launch traced here: 1850 us
  waiting for transfers between devices  1420 us (76%)
  matrix products  151 us (8%)
  local copies, waits for them, and re-layouts  150 us (8%)
  other arithmetic  74.9 us (4%)
  blocking collectives  31.4 us (2%)
    unnamed x28, waiting for transfers between devices  598 us
    reduce_scatter x1, waiting for transfers between devices, on_device(): lax.psum_scatter(expert_up_grad, 'dp', scatter_dimension=2, tiled=True)  274 us
    reduce_scatter x1, waiting for transfers between devices, on_device(): lax.psum_scatter(key_grad, 'dp', scatter_dimension=1, tiled=True)  66.8 us
    reduce_scatter x1, waiting for transfers between devices, on_device(): lax.psum_scatter(query_weight_grad, 'dp', scatter_dimension=1, tiled=True)  66.3 us
    reduce_scatter x1, waiting for transfers between devices, on_device(): lax.psum_scatter(value_grad, 'dp', scatter_dimension=1, tiled=True)  62.2 us
    all_gather x2, waiting for transfers between devices, layer_backward_pass(): lax.all_gather(back_share, 'tensor', axis=1, tiled=True)  56.6 us
    reduce_scatter x2, waiting for transfers between devices, forward_layer(): lax.psum_scatter(partial_value, 'tensor', scatter_dimension=1, tiled=True)  55.1 us
    reduce_scatter x2, waiting for transfers between devices, layer_backward_pass(): lax.psum_scatter(dispatch_grad[expert_pick, expert_slot_index], 'tensor',...  52.4 us
  transfers between devices with their start and end apart: 24, of which 23 were waited for; matrix products, arithmetic and copies ran while one was open for 10% of the time, Pallas kernels for 0%

commit v1 on v0

--- a/solution.py
+++ b/solution.py
@@ -11,6 +11,7 @@
 
 LIMITS = (12, 16, 23, 32, 46, 64, 91)
 EPSILON = 1e-06
+CAP_PADDED = 176
 PRECISE = lax.Precision.HIGHEST
 
 
@@ -51,6 +52,70 @@
     return jnp.where(alive_rows & (position < CAP), position, CAP)
 
 
+def exchange_sum(partial_value):
+    tensor_size = lax.axis_size("tensor")
+    total = partial_value
+    for shift in range(1, tensor_size):
+        pairs = [(at, (at + shift) % tensor_size) for at in range(tensor_size)]
+        total = total + lax.ppermute(partial_value, "tensor", pairs)
+    return total
+
+
+def flip_pairs(size, bit):
+    return [(at, at ^ (1 << bit)) for at in range(size)]
+
+
+def relative_order(model_width):
+    size = lax.axis_size("dp")
+    bit_count = size.bit_length() - 1
+    width = model_width // size
+    column = jnp.arange(model_width, dtype=jnp.int32)
+    place = column // width
+    mask = sum(((place >> (bit_count - 1 - bit)) & 1) << bit for bit in range(bit_count))
+    source = (mask ^ lax.axis_index("dp")) * width + column % width
+    return (column[:, None] == source[None, :]).astype(jnp.bfloat16)
+
+
+def scatter_sum(term_of, model_width):
+    size = lax.axis_size("dp")
+    bit_count = size.bit_length() - 1
+    half = model_width // 2
+    received = lax.ppermute(term_of(half, model_width), "dp", flip_pairs(size, 0))
+    if bit_count == 1:
+        return term_of(0, half) + received
+    quarter = half // 2
+    sent = term_of(quarter, half) + received[..., quarter:, :]
+    kept = term_of(0, quarter) + received[..., :quarter, :]
+    for bit in range(1, bit_count):
+        received = lax.ppermute(sent, "dp", flip_pairs(size, bit))
+        if bit == bit_count - 1:
+            return kept + received
+        middle_row = kept.shape[-2] // 2
+        sent = kept[..., middle_row:, :] + received[..., middle_row:, :]
+        kept = kept[..., :middle_row, :] + received[..., :middle_row, :]
+
+
+def doubling_sum(values):
+    size = lax.axis_size("dp")
+    for bit in range(size.bit_length() - 1):
+        values = values + lax.ppermute(values, "dp", flip_pairs(size, bit))
+    return values
+
+
+def rows_of_slots(slot_indicator, slot_rows):
+    upper = lax.reduce_precision(slot_rows, 8, 7)
+    lower = slot_rows - upper
+    return sum(
+        jnp.einsum(
+            "kt,kd->td",
+            slot_indicator,
+            part.astype(jnp.bfloat16),
+            preferred_element_type=jnp.float32,
+        )
+        for part in (upper, lower)
+    )
+
+
 def attention_scores(query_rows, key_rows, bucket_bias_table, segment, bucket_indicator):
     row_count = query_rows.shape[0]
     heads_here = bucket_bias_table.shape[1]
@@ -68,7 +133,7 @@
 
 
 def forward_layer(
-    stream, weight_set, segment, expert_pick, expert_slot_index, sources, bucket_indicator
+    stream, weight_set, segment, expert_pick, slot_indicator, bucket_indicator
 ):
     (
         query_weight,
@@ -105,8 +170,7 @@
     )
     log_total = row_peak + jnp.log(row_total)
     partial_value = jnp.dot(mixed_heads, output_weight, preferred_element_type=jnp.float32)
-    attn_share = lax.psum_scatter(partial_value, "tensor", scatter_dimension=1, tiled=True)
-    middle = stream + lax.all_gather(attn_share, "tensor", axis=1, tiled=True)
+    middle = stream + exchange_sum(partial_value)
     second = rms_norm(middle, midnorm_gain.astype(jnp.float32)).astype(jnp.bfloat16)
     logits = jnp.dot(second, router_weight, preferred_element_type=jnp.float32)
     router_probs = jax.nn.softmax(logits, axis=-1)
@@ -114,20 +178,15 @@
         jnp.float32
     )
     gate_prob = jnp.sum(router_probs * picked_expert, axis=-1, keepdims=True)
-    padded = jnp.concatenate([second, jnp.zeros((1, model_width), jnp.bfloat16)], axis=0)
-    dispatched = padded[sources]
+    dispatched = jnp.dot(slot_indicator, second).reshape(EXPERTS, CAP_PADDED, model_width)
     hidden = jnp.einsum("ecd,edf->ecf", dispatched, expert_up, preferred_element_type=jnp.float32)
     active = gelu_tanh(hidden).astype(jnp.bfloat16)
     expert_rows = jnp.einsum(
         "ecf,efd->ecd", active, expert_down, preferred_element_type=jnp.float32
     )
-    expert_rows = jnp.concatenate(
-        [expert_rows, jnp.zeros((EXPERTS, 1, model_width), jnp.float32)], axis=1
-    )
-    expert_share = lax.psum_scatter(
-        expert_rows[expert_pick, expert_slot_index], "tensor", scatter_dimension=1, tiled=True
-    )
-    combined = lax.all_gather(expert_share, "tensor", axis=1, tiled=True)
+    combined = exchange_sum(
+        rows_of_slots(slot_indicator, expert_rows.reshape(-1, model_width))
+    )
     saved_state = (
         stream,
         normed,
@@ -154,9 +213,9 @@
     weight_set,
     segment,
     expert_pick,
-    expert_slot_index,
-    sources,
+    slot_indicator,
     bucket_indicator,
+    order,
 ):
     (
         query_weight,
@@ -197,34 +256,40 @@
     logit_grad = gate_grad * gate_prob * (picked_expert - router_probs)
     router_term = jnp.dot(second.astype(jnp.float32).T, logit_grad, precision=PRECISE)
     second_grad = jnp.dot(logit_grad, router_weight.astype(jnp.float32).T, precision=PRECISE)
-    padded = jnp.concatenate([combined_grad, jnp.zeros((1, model_width), jnp.bfloat16)], axis=0)
-    slot_grad = padded[sources]
-    down_term = jnp.einsum("ecf,ecd->efd", active, slot_grad, preferred_element_type=jnp.float32)
+    slot_grad = jnp.dot(slot_indicator, combined_grad).reshape(EXPERTS, CAP_PADDED, model_width)
     active_grad = jnp.einsum(
         "ecd,efd->ecf", slot_grad, expert_down, preferred_element_type=jnp.float32
     )
     hidden_grad = jax.vjp(gelu_tanh, hidden)[1](active_grad)[0].astype(jnp.bfloat16)
-    up_term = jnp.einsum(
-        "ecd,ecf->edf", dispatched, hidden_grad, preferred_element_type=jnp.float32
-    )
     dispatch_grad = jnp.einsum(
         "ecf,edf->ecd", hidden_grad, expert_up, preferred_element_type=jnp.float32
     )
-    dispatch_grad = jnp.concatenate(
-        [dispatch_grad, jnp.zeros((EXPERTS, 1, model_width), jnp.float32)], axis=1
-    )
-    back_share = lax.psum_scatter(
-        dispatch_grad[expert_pick, expert_slot_index], "tensor", scatter_dimension=1, tiled=True
-    )
-    second_grad = second_grad + lax.all_gather(back_share, "tensor", axis=1, tiled=True)
+    second_grad = second_grad + exchange_sum(
+        rows_of_slots(slot_indicator, dispatch_grad.reshape(-1, model_width))
+    )
+    slot_grad_ordered = jnp.dot(slot_grad, order)
+    dispatched_ordered = jnp.dot(dispatched, order)
+
+    def expert_term(ordered, hidden_rows):
+        def term_of(low, high):
+            return jnp.einsum(
+                "cd,cf->df", ordered[:, low:high], hidden_rows, preferred_element_type=jnp.float32
+            )
+
+        return scatter_sum(term_of, model_width)
+
+    down_term = jnp.stack(
+        [expert_term(slot_grad_ordered[at], active[at]).T for at in range(EXPERTS)]
+    )
+    up_term = jnp.stack(
+        [expert_term(dispatched_ordered[at], hidden_grad[at]) for at in range(EXPERTS)]
+    )
     middle_grad, midnorm_term = jax.vjp(rms_norm, middle, midnorm_gain.astype(jnp.float32))[1](
         second_grad
     )
     middle_grad = upstream + middle_grad
     attn_grad = middle_grad.astype(jnp.bfloat16)
-    output_term = jnp.einsum(
-        "tf,td->fd", mixed_heads, attn_grad, preferred_element_type=jnp.float32
-    )
+    output_term = expert_term(jnp.dot(attn_grad, order), mixed_heads).T
     mixed_grad = jnp.einsum(
         "td,fd->tf", attn_grad, output_weight, preferred_element_type=jnp.float32
     ).astype(jnp.bfloat16)
@@ -255,16 +320,16 @@
     query_back = query_back.reshape(row_count, -1).astype(jnp.bfloat16)
     key_back = key_back.reshape(row_count, -1).astype(jnp.bfloat16)
     value_back = value_back.reshape(row_count, -1).astype(jnp.bfloat16)
-    query_term = jnp.einsum("td,tf->df", normed, query_back, preferred_element_type=jnp.float32)
-    key_term = jnp.einsum("td,tf->df", normed, key_back, preferred_element_type=jnp.float32)
-    value_term = jnp.einsum("td,tf->df", normed, value_back, preferred_element_type=jnp.float32)
+    projection_term = expert_term(
+        jnp.dot(normed, order), jnp.concatenate([query_back, key_back, value_back], axis=1)
+    )
+    query_term, key_term, value_term = jnp.split(projection_term, 3, axis=1)
     normed_part = (
         jnp.einsum("tf,df->td", query_back, query_weight, preferred_element_type=jnp.float32)
         + jnp.einsum("tf,df->td", key_back, key_weight, preferred_element_type=jnp.float32)
         + jnp.einsum("tf,df->td", value_back, value_weight, preferred_element_type=jnp.float32)
     )
-    normed_share = lax.psum_scatter(normed_part, "tensor", scatter_dimension=1, tiled=True)
-    normed_grad = lax.all_gather(normed_share, "tensor", axis=1, tiled=True)
+    normed_grad = exchange_sum(normed_part)
     stream_grad, prenorm_term = jax.vjp(rms_norm, stream, prenorm_gain.astype(jnp.float32))[1](
         normed_grad
     )
@@ -303,11 +368,13 @@
     segment, alive_rows = segments(lengths[0], row_count)
     expert_pick = expert_ids[:, 0]
     expert_slot_index = slot_of(expert_pick, alive_rows)
-    sources = (
-        jnp.full((EXPERTS, CAP + 1), row_count, jnp.int32)
-        .at[expert_pick, expert_slot_index]
-        .set(jnp.arange(row_count, dtype=jnp.int32))[:, :CAP]
-    )
+    flat_slot = jnp.where(
+        expert_slot_index < CAP, expert_pick * CAP_PADDED + expert_slot_index, -1
+    )
+    slot_indicator = (
+        jnp.arange(EXPERTS * CAP_PADDED, dtype=jnp.int32)[:, None] == flat_slot[None, :]
+    ).astype(jnp.bfloat16)
+    order = relative_order(tokens.shape[1])
     position = jnp.arange(row_count, dtype=jnp.int32)
     bucket_map = bucket_ids(position, position)
     bucket_indicator = (
@@ -330,7 +397,7 @@
     for layer_index in range(LAYERS):
         weight_set = tuple((weight_arr[layer_index] for weight_arr in weight_all))
         saved_state, stream = forward_layer(
-            stream, weight_set, segment, expert_pick, expert_slot_index, sources, bucket_indicator
+            stream, weight_set, segment, expert_pick, slot_indicator, bucket_indicator
         )
         saved_list.append(saved_state)
     upstream = cotangent.astype(jnp.float32) * alive_rows[:, None].astype(jnp.float32)
@@ -343,9 +410,9 @@
             weight_set,
             segment,
             expert_pick,
-            expert_slot_index,
-            sources,
+            slot_indicator,
             bucket_indicator,
+            order,
         )
         layer_terms[layer_index] = term_set
     (
@@ -365,28 +432,30 @@
             for member in range(10)
         )
     )
-    (
-        query_weight_grad,
-        key_grad,
-        value_grad,
-        output_grad,
-        prenorm_grad,
-        midnorm_grad,
-        router_grad,
-        expert_up_grad,
-        down_grad,
-    ) = (
-        lax.psum_scatter(query_weight_grad, "dp", scatter_dimension=1, tiled=True),
-        lax.psum_scatter(key_grad, "dp", scatter_dimension=1, tiled=True),
-        lax.psum_scatter(value_grad, "dp", scatter_dimension=1, tiled=True),
-        lax.psum_scatter(output_grad, "dp", scatter_dimension=2, tiled=True),
-        lax.psum_scatter(prenorm_grad, "dp", scatter_dimension=1, tiled=True),
-        lax.psum_scatter(midnorm_grad, "dp", scatter_dimension=1, tiled=True),
-        lax.psum_scatter(router_grad, "dp", scatter_dimension=1, tiled=True),
-        lax.psum_scatter(expert_up_grad, "dp", scatter_dimension=2, tiled=True),
-        lax.psum_scatter(down_grad, "dp", scatter_dimension=3, tiled=True),
-    )
-    table_grad = lax.psum(table_grad, "dp")
+    model_width = tokens.shape[1]
+    heads_here = bucket_bias_table.shape[2]
+    small = jnp.concatenate(
+        [
+            prenorm_grad,
+            midnorm_grad,
+            router_grad.transpose(2, 0, 1).reshape(EXPERTS * LAYERS, model_width),
+            jnp.pad(
+                table_grad.reshape(LAYERS, -1),
+                ((0, 0), (0, model_width - POSITION_BUCKETS * heads_here)),
+            ),
+        ]
+    )
+    small = doubling_sum(small)
+    width = model_width // lax.axis_size("dp")
+    own = lax.dynamic_slice_in_dim(
+        small[: (2 + EXPERTS) * LAYERS], lax.axis_index("dp") * width, width, axis=1
+    )
+    prenorm_grad = own[:LAYERS]
+    midnorm_grad = own[LAYERS : 2 * LAYERS]
+    router_grad = own[2 * LAYERS :].reshape(EXPERTS, LAYERS, width).transpose(1, 2, 0)
+    table_grad = small[(2 + EXPERTS) * LAYERS :, : POSITION_BUCKETS * heads_here].reshape(
+        LAYERS, POSITION_BUCKETS, heads_here
+    )
     return (
         stream.astype(jnp.bfloat16),
         upstream,

time: 1860 us -> 980 us (0.53)
  waiting for transfers between devices: 1420 us -> 574 us
  local copies, waits for them, and re-layouts: 150 us -> 28.4 us
  matrix products: 151 us -> 231 us
  starting transfers between devices: 3.39 us -> 83 us
  blocking collectives: 31.4 us -> 0 us
  other arithmetic: 74.9 us -> 55.5 us
    reduce_scatter x12 -> x0, waiting for transfers between devices: 661 us -> none  [the longest x1 274 us: on_device(): lax.psum_scatter(expert_up_grad, 'dp', scatter_dimension=2, tiled=True)]
    unnamed x28 -> x0, waiting for transfers between devices: 598 us -> none
    ppermute x0 -> x76, waiting for transfers between devices: none -> 574 us  [the longest x48 396 us: scatter_sum(): received = lax.ppermute(sent, 'dp', flip_pairs(size, bit))]
    all_gather x8 -> x0, waiting for transfers between devices: 161 us -> none  [the longest x2 56.6 us: layer_backward_pass(): lax.all_gather(back_share, 'tensor', axis=1, tiled=True)]
    dot_general x12 -> x68, matrix products: 30 us -> 117 us  [the longest x48 95.5 us: term_of(): jnp.einsum('cd,cf->df', ordered[:, low:high], hidden_rows, preferred_elem...]
    ppermute x0 -> x76, starting transfers between devices: none -> 83 us  [the longest x48 61 us: scatter_sum(): received = lax.ppermute(sent, 'dp', flip_pairs(size, bit))]
    another operation x2 -> x4, local copies, waits for them, and re-layouts: 47.3 us -> 2.19 us  [on_device(): jnp.stack([layer_terms[layer_index][member] for layer_index in range(LAYE...]
    gather x12 -> x0, local copies, waits for them, and re-layouts: 42.8 us -> none  [the longest x2 14.8 us: layer_backward_pass(): dispatch_grad[expert_pick, expert_slot_index]]
  transfers between devices with their start and end apart: 24 -> 76, of which waited for: 23 -> 41; matrix products, arithmetic and copies ran while one was open for 10% -> 25% of each run, Pallas kernels for 0% -> 0%
where the time goes in v1:
time: 980 us; the launch traced here: 976 us
  waiting for transfers between devices  574 us (59%)
  matrix products  231 us (24%)
  starting transfers between devices  83 us (8%)
  other arithmetic  55.5 us (6%)
  local copies, waits for them, and re-layouts  28.4 us (3%)
    ppermute x48, waiting for transfers between devices, scatter_sum(): received = lax.ppermute(sent, 'dp', flip_pairs(size, bit))  396 us
    ppermute x8, waiting for transfers between devices, exchange_sum(): total = total + lax.ppermute(partial_value, 'tensor', pairs)  127 us
    dot_general x48, matrix products, term_of(): jnp.einsum('cd,cf->df', ordered[:, low:high], hidden_rows, preferred_elem...  95.5 us
    ppermute x48, starting transfers between devices, scatter_sum(): received = lax.ppermute(sent, 'dp', flip_pairs(size, bit))  61 us
    ppermute x4, waiting for transfers between devices, doubling_sum(): values = values + lax.ppermute(values, 'dp', flip_pairs(size, bit))  50.3 us
  transfers between devices with their start and end apart: 76, of which 41 were waited for; matrix products, arithmetic and copies ran while one was open for 25% of the time, Pallas kernels for 0%

profile of v1, /device:TPU:0, one launch (start us, length us, event | category | flops | bytes accessed | tf_op | source)
XLA Modules:
  0.0 975.6 jit_solution(3764639629896161939)
XLA Ops:
  30.7 33.8 %collective-permute-done = f32[512,768]{1,0:T(8,128)S(1)} collective-permute-done((f32[512,768]{1,0:T(8,128)S(1)}, f32[512,768]{1,0:T(8,128)S(1)}, u32[]{:S(2)}, u32[]{:S(2)}) %collective-permute-start) | collective-permute-done | bytes 1572896 | tf_op jit(solution)/shard_map/ppermute | solution.py:60
  85.2 27.9 %collective-permute-done.1 = f32[512,768]{1,0:T(8,128)} collective-permute-done((f32[512,768]{1,0:T(8,128)}, f32[512,768]{1,0:T(8,128)}, u32[]{:S(2)}, u32[]{:S(2)}) %collective-permute-start.1) | collective-permute-done | bytes 1572896 | tf_op jit(solution)/shard_map/ppermute | solution.py:60
  135.8 27.0 %collective-permute-done.2 = f32[512,768]{1,0:T(8,128)S(1)} collective-permute-done((f32[512,768]{1,0:T(8,128)S(1)}, f32[512,768]{1,0:T(8,128)S(1)}, u32[]{:S(2)}, u32[]{:S(2)}) %collective-permute-start.2) | collective-permute-done | bytes 1572896 | tf_op jit(solution)/shard_map/ppermute | solution.py:60
  217.1 28.6 %collective-permute-done.4 = f32[512,768]{1,0:T(8,128)S(1)} collective-permute-done((f32[512,768]{1,0:T(8,128)S(1)}, f32[512,768]{1,0:T(8,128)S(1)}, u32[]{:S(2)}, u32[]{:S(2)}) %collective-permute-start.4) | collective-permute-done | bytes 1572896 | tf_op jit(solution)/shard_map/ppermute | solution.py:60
  369.5 19.8 %collective-permute-done.41 = f32[192,1536]{1,0:T(8,128)} collective-permute-done((f32[192,1536]{1,0:T(8,128)}, f32[192,1536]{1,0:T(8,128)}, u32[]{:S(2)}, u32[]{:S(2)}) %collective-permute-start.41) | collective-permute-done | bytes 1179680 | tf_op jit(solution)/shard_map/ppermute | solution.py:90
  390.7 23.8 %collective-permute-done.73 = f32[192,1536]{1,0:T(8,128)} collective-permute-done((f32[192,1536]{1,0:T(8,128)}, f32[192,1536]{1,0:T(8,128)}, u32[]{:S(2)}, u32[]{:S(2)}) %collective-permute-start.73) | collective-permute-done | bytes 1179680 | tf_op jit(solution)/shard_map/ppermute | solution.py:90
  416.0 23.7 %collective-permute-done.69 = f32[192,1536]{1,0:T(8,128)S(1)} collective-permute-done((f32[192,1536]{1,0:T(8,128)}, f32[192,1536]{1,0:T(8,128)S(1)}, u32[]{:S(2)}, u32[]{:S(2)}) %collective-permute-start.69) | collective-permute-done | bytes 1179680 | tf_op jit(solution)/shard_map/ppermute | solution.py:90
  441.5 22.7 %collective-permute-done.65 = f32[192,1536]{1,0:T(8,128)S(1)} collective-permute-done((f32[192,1536]{1,0:T(8,128)S(1)}, f32[192,1536]{1,0:T(8,128)S(1)}, u32[]{:S(2)}, u32[]{:S(2)}) %collective-permute-start.65) | collective-permute-done | bytes 1179680 | tf_op jit(solution)/shard_map/ppermute | solution.py:90
  466.4 14.0 %collective-permute-done.46 = f32[96,1536]{1,0:T(8,128)S(1)} collective-permute-done((f32[96,1536]{1,0:T(8,128)S(1)}, f32[96,1536]{1,0:T(8,128)S(1)}, u32[]{:S(2)}, u32[]{:S(2)}) %collective-permute-start.46) | collective-permute-done | bytes 589856 | tf_op jit(solution)/shard_map/ppermute | solution.py:90
  482.0 11.0 %collective-permute-done.42 = f32[96,1536]{1,0:T(8,128)S(1)} collective-permute-done((f32[96,1536]{1,0:T(8,128)S(1)}, f32[96,1536]{1,0:T(8,128)S(1)}, u32[]{:S(2)}, u32[]{:S(2)}) %collective-permute-start.42) | collective-permute-done | bytes 589856 | tf_op jit(solution)/shard_map/ppermute | solution.py:90
  494.6 11.0 %collective-permute-done.74 = f32[96,1536]{1,0:T(8,128)S(1)} collective-permute-done((f32[96,1536]{1,0:T(8,128)S(1)}, f32[96,1536]{1,0:T(8,128)S(1)}, u32[]{:S(2)}, u32[]{:S(2)}) %collective-permute-start.74) | collective-permute-done | bytes 589856 | tf_op jit(solution)/shard_map/ppermute | solution.py:90
  507.3 11.0 %collective-permute-done.70 = f32[96,1536]{1,0:T(8,128)S(1)} collective-permute-done((f32[96,1536]{1,0:T(8,128)S(1)}, f32[96,1536]{1,0:T(8,128)S(1)}, u32[]{:S(2)}, u32[]{:S(2)}) %collective-permute-start.70) | collective-permute-done | bytes 589856 | tf_op jit(solution)/shard_map/ppermute | solution.py:90
  548.7 11.0 %collective-permute-done.47 = f32[48,1536]{1,0:T(8,128)S(1)} collective-permute-done((f32[48,1536]{1,0:T(8,128)S(1)}, f32[48,1536]{1,0:T(8,128)S(1)}, u32[]{:S(2)}, u32[]{:S(2)}) %collective-permute-start.47) | collective-permute-done | bytes 294944 | tf_op jit(solution)/shard_map/ppermute | solution.py:90
  559.7 13.4 %collective-permute-done.43 = f32[48,1536]{1,0:T(8,128)S(1)} collective-permute-done((f32[48,1536]{1,0:T(8,128)S(1)}, f32[48,1536]{1,0:T(8,128)S(1)}, u32[]{:S(2)}, u32[]{:S(2)}) %collective-permute-start.43) | collective-permute-done | bytes 294944 | tf_op jit(solution)/shard_map/ppermute | solution.py:90
  573.2 16.1 %collective-permute-done.75 = f32[48,1536]{1,0:T(8,128)S(1)} collective-permute-done((f32[48,1536]{1,0:T(8,128)S(1)}, f32[48,1536]{1,0:T(8,128)S(1)}, u32[]{:S(2)}, u32[]{:S(2)}) %collective-permute-start.75) | collective-permute-done | bytes 294944 | tf_op jit(solution)/shard_map/ppermute | solution.py:90
  589.4 14.6 %collective-permute-done.71 = f32[48,1536]{1,0:T(8,128)S(1)} collective-permute-done((f32[48,1536]{1,0:T(8,128)S(1)}, f32[48,1536]{1,0:T(8,128)S(1)}, u32[]{:S(2)}, u32[]{:S(2)}) %collective-permute-start.71) | collective-permute-done | bytes 294944 | tf_op jit(solution)/shard_map/ppermute | solution.py:90
  604.1 15.9 %collective-permute-done.67 = f32[48,1536]{1,0:T(8,128)S(1)} collective-permute-done((f32[48,1536]{1,0:T(8,128)S(1)}, f32[48,1536]{1,0:T(8,128)S(1)}, u32[]{:S(2)}, u32[]{:S(2)}) %collective-permute-start.67) | collective-permute-done | bytes 294944 | tf_op jit(solution)/shard_map/ppermute | solution.py:90
  729.8 48.2 %collective-permute-done.25 = f32[12,768]{1,0:T(8,128)S(1)} collective-permute-done((f32[12,768]{1,0:T(8,128)S(1)}, f32[12,768]{1,0:T(8,128)S(1)}, u32[]{:S(2)}, u32[]{:S(2)}) %collective-permute-start.25) | collective-permute-done | bytes 36896 | tf_op jit(solution)/shard_map/ppermute | solution.py:101
  804.0 12.8 %collective-permute-done.61 = f32[192,1536]{1,0:T(8,128)S(1)} collective-permute-done((f32[192,1536]{1,0:T(8,128)}, f32[192,1536]{1,0:T(8,128)S(1)}, u32[]{:S(2)}, u32[]{:S(2)}) %collective-permute-start.61) | collective-permute-done | bytes 1179680 | tf_op jit(solution)/shard_map/ppermute | solution.py:90
  818.3 23.8 %collective-permute-done.57 = f32[192,1536]{1,0:T(8,128)S(1)} collective-permute-done((f32[192,1536]{1,0:T(8,128)}, f32[192,1536]{1,0:T(8,128)S(1)}, u32[]{:S(2)}, u32[]{:S(2)}) %collective-permute-start.57) | collective-permute-done | bytes 1179680 | tf_op jit(solution)/shard_map/ppermute | solution.py:90
  843.6 23.8 %collective-permute-done.53 = f32[192,1536]{1,0:T(8,128)S(1)} collective-permute-done((f32[192,1536]{1,0:T(8,128)S(1)}, f32[192,1536]{1,0:T(8,128)S(1)}, u32[]{:S(2)}, u32[]{:S(2)}) %collective-permute-start.53) | collective-permute-done | bytes 1179680 | tf_op jit(solution)/shard_map/ppermute | solution.py:90
  872.4 17.5 %collective-permute-done.62 = f32[96,1536]{1,0:T(8,128)S(1)} collective-permute-done((f32[96,1536]{1,0:T(8,128)S(1)}, f32[96,1536]{1,0:T(8,128)S(1)}, u32[]{:S(2)}, u32[]{:S(2)}) %collective-permute-start.62) | collective-permute-done | bytes 589856 | tf_op jit(solution)/shard_map/ppermute | solution.py:90
  890.0 18.9 %collective-permute-done.58 = f32[96,1536]{1,0:T(8,128)S(1)} collective-permute-done((f32[96,1536]{1,0:T(8,128)S(1)}, f32[96,1536]{1,0:T(8,128)S(1)}, u32[]{:S(2)}, u32[]{:S(2)}) %collective-permute-start.58) | collective-permute-done | bytes 589856 | tf_op jit(solution)/shard_map/ppermute | solution.py:90
  923.9 22.5 %collective-permute-done.31 = f32[48,1536]{1,0:T(8,128)S(1)} collective-permute-done((f32[48,1536]{1,0:T(8,128)S(1)}, f32[48,1536]{1,0:T(8,128)S(1)}, u32[]{:S(2)}, u32[]{:S(2)}) %collective-permute-start.31) | collective-permute-done | bytes 294944 | tf_op jit(solution)/shard_map/ppermute | solution.py:90
  (787 shorter events, 478.8 us)
Async XLA Ops:
  200.1 85.0 %collective-permute-start.48 = (f32[384,1536]{1,0:T(8,128)}, f32[384,1536]{1,0:T(8,128)}, u32[]{:S(2)}, u32[]{:S(2)}) collective-permute-start(f32[384,1536]{1,0:T(8,128)} %fusion.202), channel_id=1, source_target_pairs={{0,2},{2,0},{4,6},{6,4},{8,10},{10,8},{12,14},{14,12},{16,18},{18,... | collective-permute-start | bytes 7077896 | tf_op jit(solution)/shard_map/ppermute | solution.py:83
  202.1 88.7 %collective-permute-start.44 = (f32[384,1536]{1,0:T(8,128)}, f32[384,1536]{1,0:T(8,128)}, u32[]{:S(2)}, u32[]{:S(2)}) collective-permute-start(f32[384,1536]{1,0:T(8,128)} %fusion.199), channel_id=1, source_target_pairs={{0,2},{2,0},{4,6},{6,4},{8,10},{10,8},{12,14},{14,12},{16,18},{18,... | collective-permute-start | bytes 7077896 | tf_op jit(solution)/shard_map/ppermute | solution.py:83
  204.5 92.5 %collective-permute-start.40 = (f32[384,1536]{1,0:T(8,128)}, f32[384,1536]{1,0:T(8,128)}, u32[]{:S(2)}, u32[]{:S(2)}) collective-permute-start(f32[384,1536]{1,0:T(8,128)} %fusion.196), channel_id=1, source_target_pairs={{0,2},{2,0},{4,6},{6,4},{8,10},{10,8},{12,14},{14,12},{16,18},{18,... | collective-permute-start | bytes 7077896 | tf_op jit(solution)/shard_map/ppermute | solution.py:83
  215.6 87.1 %collective-permute-start.72 = (f32[384,1536]{1,0:T(8,128)}, f32[384,1536]{1,0:T(8,128)}, u32[]{:S(2)}, u32[]{:S(2)}) collective-permute-start(f32[384,1536]{1,0:T(8,128)} %fusion.220), channel_id=1, source_target_pairs={{0,2},{2,0},{4,6},{6,4},{8,10},{10,8},{12,14},{14,12},{16,18},{18,... | collective-permute-start | bytes 7077896 | tf_op jit(solution)/shard_map/ppermute | solution.py:83
  297.0 61.6 %collective-permute-start.12 = (f32[384,1152]{1,0:T(8,128)}, f32[384,1152]{1,0:T(8,128)}, u32[]{:S(2)}, u32[]{:S(2)}) collective-permute-start(f32[384,1152]{1,0:T(8,128)} %fusion.226), channel_id=1, source_target_pairs={{0,2},{2,0},{4,6},{6,4},{8,10},{10,8},{12,14},{14,12},{16,18},{18,... | collective-permute-start | bytes 5308424 | tf_op jit(solution)/shard_map/ppermute | solution.py:83
  309.6 54.6 %collective-permute-start.49 = (f32[192,1536]{1,0:T(8,128)}, f32[192,1536]{1,0:T(8,128)}, u32[]{:S(2)}, u32[]{:S(2)}) collective-permute-start(f32[192,1536]{1,0:T(8,128)} %slice_add_fusion.12), channel_id=1, source_target_pairs={{0,4},{2,6},{4,0},{6,2},{8,12},{10,14},{12,8},{14,10},{16,20},{18,... | collective-permute-start | bytes 3538952 | tf_op jit(solution)/shard_map/ppermute | solution.py:90
  313.0 53.4 %collective-permute-start.45 = (f32[192,1536]{1,0:T(8,128)}, f32[192,1536]{1,0:T(8,128)}, u32[]{:S(2)}, u32[]{:S(2)}) collective-permute-start(f32[192,1536]{1,0:T(8,128)} %slice_add_fusion.14), channel_id=1, source_target_pairs={{0,4},{2,6},{4,0},{6,2},{8,12},{10,14},{12,8},{14,10},{16,20},{18,... | collective-permute-start | bytes 3538952 | tf_op jit(solution)/shard_map/ppermute | solution.py:90
  325.3 64.0 %collective-permute-start.41 = (f32[192,1536]{1,0:T(8,128)}, f32[192,1536]{1,0:T(8,128)}, u32[]{:S(2)}, u32[]{:S(2)}) collective-permute-start(f32[192,1536]{1,0:T(8,128)} %slice_add_fusion.16), channel_id=1, source_target_pairs={{0,4},{2,6},{4,0},{6,2},{8,12},{10,14},{12,8},{14,10},{16,20},{18,... | collective-permute-start | bytes 3538952 | tf_op jit(solution)/shard_map/ppermute | solution.py:90
  327.5 87.0 %collective-permute-start.73 = (f32[192,1536]{1,0:T(8,128)}, f32[192,1536]{1,0:T(8,128)}, u32[]{:S(2)}, u32[]{:S(2)}) collective-permute-start(f32[192,1536]{1,0:T(8,128)} %slice_add_fusion), channel_id=1, source_target_pairs={{0,4},{2,6},{4,0},{6,2},{8,12},{10,14},{12,8},{14,10},{16,20},{18,... | collective-permute-start | bytes 3538952 | tf_op jit(solution)/shard_map/ppermute | solution.py:90
  358.6 81.2 %collective-permute-start.69 = (f32[192,1536]{1,0:T(8,128)}, f32[192,1536]{1,0:T(8,128)S(1)}, u32[]{:S(2)}, u32[]{:S(2)}) collective-permute-start(f32[192,1536]{1,0:T(8,128)} %slice_add_fusion.2), channel_id=1, source_target_pairs={{0,4},{2,6},{4,0},{6,2},{8,12},{10,14},{12,8},{14,10},{16,20},{18,... | collective-permute-start | bytes 3538952 | tf_op jit(solution)/shard_map/ppermute | solution.py:90
  364.2 99.9 %collective-permute-start.65 = (f32[192,1536]{1,0:T(8,128)S(1)}, f32[192,1536]{1,0:T(8,128)S(1)}, u32[]{:S(2)}, u32[]{:S(2)}) collective-permute-start(f32[192,1536]{1,0:T(8,128)S(1)} %copy-done.111), channel_id=1, source_target_pairs={{0,4},{2,6},{4,0},{6,2},{8,12},{10,14},{12,8},{14,10},{16,20},{18,... | collective-permute-start | bytes 3538952 | tf_op jit(solution)/shard_map/ppermute | solution.py:90
  366.4 270.3 %collective-permute-start.6 = (f32[512,768]{1,0:T(8,128)S(1)}, f32[512,768]{1,0:T(8,128)S(1)}, u32[]{:S(2)}, u32[]{:S(2)}) collective-permute-start(f32[512,768]{1,0:T(8,128)S(1)} %convolution_add_fusion), channel_id=1, source_target_pairs={{0,1},{1,0},{2,3},{3,2},{4,5},{5,4},{6,7},{7,6},{8,9},{9,8},{10,11... | collective-permute-start | bytes 4718600 | tf_op jit(solution)/shard_map/ppermute | solution.py:60
  389.3 282.5 %collective-permute-start.36 = (f32[384,1536]{1,0:T(8,128)}, f32[384,1536]{1,0:T(8,128)}, u32[]{:S(2)}, u32[]{:S(2)}) collective-permute-start(f32[384,1536]{1,0:T(8,128)} %fusion.193), channel_id=1, source_target_pairs={{0,2},{2,0},{4,6},{6,4},{8,10},{10,8},{12,14},{14,12},{16,18},{18,... | collective-permute-start | bytes 7077896 | tf_op jit(solution)/shard_map/ppermute | solution.py:83
  414.5 262.9 %collective-permute-start.32 = (f32[384,1536]{1,0:T(8,128)}, f32[384,1536]{1,0:T(8,128)}, u32[]{:S(2)}, u32[]{:S(2)}) collective-permute-start(f32[384,1536]{1,0:T(8,128)} %fusion.190), channel_id=1, source_target_pairs={{0,2},{2,0},{4,6},{6,4},{8,10},{10,8},{12,14},{14,12},{16,18},{18,... | collective-permute-start | bytes 7077896 | tf_op jit(solution)/shard_map/ppermute | solution.py:83
  529.1 155.8 %collective-permute-start.28 = (f32[384,1536]{1,0:T(8,128)}, f32[384,1536]{1,0:T(8,128)}, u32[]{:S(2)}, u32[]{:S(2)}) collective-permute-start(f32[384,1536]{1,0:T(8,128)} %fusion.187), channel_id=1, source_target_pairs={{0,2},{2,0},{4,6},{6,4},{8,10},{10,8},{12,14},{14,12},{16,18},{18,... | collective-permute-start | bytes 7077896 | tf_op jit(solution)/shard_map/ppermute | solution.py:83
  636.0 54.5 %collective-permute-start.60 = (f32[384,1536]{1,0:T(8,128)}, f32[384,1536]{1,0:T(8,128)}, u32[]{:S(2)}, u32[]{:S(2)}) collective-permute-start(f32[384,1536]{1,0:T(8,128)} %fusion.211), channel_id=1, source_target_pairs={{0,2},{2,0},{4,6},{6,4},{8,10},{10,8},{12,14},{14,12},{16,18},{18,... | collective-permute-start | bytes 7077896 | tf_op jit(solution)/shard_map/ppermute | solution.py:83
  684.9 105.9 %collective-permute-start.8 = (f32[384,1152]{1,0:T(8,128)}, f32[384,1152]{1,0:T(8,128)}, u32[]{:S(2)}, u32[]{:S(2)}) collective-permute-start(f32[384,1152]{1,0:T(8,128)} %fusion.228), channel_id=1, source_target_pairs={{0,2},{2,0},{4,6},{6,4},{8,10},{10,8},{12,14},{14,12},{16,18},{18,... | collective-permute-start | bytes 5308424 | tf_op jit(solution)/shard_map/ppermute | solution.py:83
  698.1 98.0 %collective-permute-start.37 = (f32[192,1536]{1,0:T(8,128)}, f32[192,1536]{1,0:T(8,128)}, u32[]{:S(2)}, u32[]{:S(2)}) collective-permute-start(f32[192,1536]{1,0:T(8,128)} %slice_add_fusion.18), channel_id=1, source_target_pairs={{0,4},{2,6},{4,0},{6,2},{8,12},{10,14},{12,8},{14,10},{16,20},{18,... | collective-permute-start | bytes 3538952 | tf_op jit(solution)/shard_map/ppermute | solution.py:90
  701.0 97.6 %collective-permute-start.33 = (f32[192,1536]{1,0:T(8,128)}, f32[192,1536]{1,0:T(8,128)}, u32[]{:S(2)}, u32[]{:S(2)}) collective-permute-start(f32[192,1536]{1,0:T(8,128)} %slice_add_fusion.20), channel_id=1, source_target_pairs={{0,4},{2,6},{4,0},{6,2},{8,12},{10,14},{12,8},{14,10},{16,20},{18,... | collective-permute-start | bytes 3538952 | tf_op jit(solution)/shard_map/ppermute | solution.py:90
  710.0 91.2 %collective-permute-start.29 = (f32[192,1536]{1,0:T(8,128)}, f32[192,1536]{1,0:T(8,128)}, u32[]{:S(2)}, u32[]{:S(2)}) collective-permute-start(f32[192,1536]{1,0:T(8,128)} %slice_add_fusion.22), channel_id=1, source_target_pairs={{0,4},{2,6},{4,0},{6,2},{8,12},{10,14},{12,8},{14,10},{16,20},{18,... | collective-permute-start | bytes 3538952 | tf_op jit(solution)/shard_map/ppermute | solution.py:90
  796.2 71.2 %collective-permute-start.53 = (f32[192,1536]{1,0:T(8,128)S(1)}, f32[192,1536]{1,0:T(8,128)S(1)}, u32[]{:S(2)}, u32[]{:S(2)}) collective-permute-start(f32[192,1536]{1,0:T(8,128)S(1)} %copy-done.110), channel_id=1, source_target_pairs={{0,4},{2,6},{4,0},{6,2},{8,12},{10,14},{12,8},{14,10},{16,20},{18,... | collective-permute-start | bytes 3538952 | tf_op jit(solution)/shard_map/ppermute | solution.py:90
  798.6 119.4 %collective-permute-start.9 = (f32[192,1152]{1,0:T(8,128)S(1)}, f32[192,1152]{1,0:T(8,128)S(1)}, u32[]{:S(2)}, u32[]{:S(2)}) collective-permute-start(f32[192,1152]{1,0:T(8,128)S(1)} %slice_add_fusion.26), channel_id=1, source_target_pairs={{0,4},{2,6},{4,0},{6,2},{8,12},{10,14},{12,8},{14,10},{16,20},{18,... | collective-permute-start | bytes 2654216 | tf_op jit(solution)/shard_map/ppermute | solution.py:90
  801.2 67.6 %collective-permute-start.38 = (f32[96,1536]{1,0:T(8,128)S(1)}, f32[96,1536]{1,0:T(8,128)S(1)}, u32[]{:S(2)}, u32[]{:S(2)}) collective-permute-start(f32[96,1536]{1,0:T(8,128)S(1)} %get-tuple-element.80), channel_id=1, source_target_pairs={{0,8},{2,10},{4,12},{6,14},{8,0},{10,2},{12,4},{14,6},{16,24},{18,... | collective-permute-start | bytes 1769480 | tf_op jit(solution)/shard_map/ppermute | solution.py:90
  816.8 52.8 %collective-permute-start.34 = (f32[96,1536]{1,0:T(8,128)S(1)}, f32[96,1536]{1,0:T(8,128)S(1)}, u32[]{:S(2)}, u32[]{:S(2)}) collective-permute-start(f32[96,1536]{1,0:T(8,128)S(1)} %get-tuple-element.78), channel_id=1, source_target_pairs={{0,8},{2,10},{4,12},{6,14},{8,0},{10,2},{12,4},{14,6},{16,24},{18,... | collective-permute-start | bytes 1769480 | tf_op jit(solution)/shard_map/ppermute | solution.py:90
  (251 other events, 3436.9 us)

commit v2 on v1

--- a/solution.py
+++ b/solution.py
@@ -76,23 +76,40 @@
     return (column[:, None] == source[None, :]).astype(jnp.bfloat16)
 
 
-def scatter_sum(term_of, model_width):
-    size = lax.axis_size("dp")
-    bit_count = size.bit_length() - 1
-    half = model_width // 2
-    received = lax.ppermute(term_of(half, model_width), "dp", flip_pairs(size, 0))
-    if bit_count == 1:
-        return term_of(0, half) + received
-    quarter = half // 2
-    sent = term_of(quarter, half) + received[..., quarter:, :]
-    kept = term_of(0, quarter) + received[..., :quarter, :]
-    for bit in range(1, bit_count):
-        received = lax.ppermute(sent, "dp", flip_pairs(size, bit))
-        if bit == bit_count - 1:
-            return kept + received
-        middle_row = kept.shape[-2] // 2
-        sent = kept[..., middle_row:, :] + received[..., middle_row:, :]
-        kept = kept[..., :middle_row, :] + received[..., :middle_row, :]
+class ScatterSum:
+    def __init__(self, term_of, model_width):
+        self.size = lax.axis_size("dp")
+        self.term_of = term_of
+        self.half = model_width // 2
+        self.sent = term_of(self.half, model_width)
+        self.kept = None
+        self.bit = 0
+
+    def step(self, after=None):
+        if self.bit == self.size.bit_length() - 1:
+            return
+        sent = self.sent
+        if after is not None:
+            sent, _ = lax.optimization_barrier((sent, after))
+        received = lax.ppermute(sent, "dp", flip_pairs(self.size, self.bit))
+        self.bit += 1
+        if self.bit == 1:
+            low_half = self.half // 2
+            self.sent = self.term_of(low_half, self.half) + received[low_half:]
+            self.kept = self.term_of(0, low_half) + received[:low_half]
+            return
+        total = (self.kept, received)
+        if self.bit == self.size.bit_length() - 1:
+            self.kept = total[0] + total[1]
+            return
+        low_half = received.shape[0] // 2
+        self.sent = total[0][low_half:] + total[1][low_half:]
+        self.kept = total[0][:low_half] + total[1][:low_half]
+
+
+def step_all(group, after=None):
+    for one in group:
+        one.step(after)
 
 
 def doubling_sum(values):
@@ -216,6 +233,7 @@
     slot_indicator,
     bucket_indicator,
     order,
+    earlier,
 ):
     (
         query_weight,
@@ -252,6 +270,9 @@
         jnp.float32
     )
     combined_grad = (gate_prob * upstream).astype(jnp.bfloat16)
+    if earlier:
+        step_all(earlier["up"], upstream[:8, :128])
+        step_all(earlier["down"], upstream[:8, :128])
     gate_grad = jnp.sum(upstream * combined, axis=-1, keepdims=True)
     logit_grad = gate_grad * gate_prob * (picked_expert - router_probs)
     router_term = jnp.dot(second.astype(jnp.float32).T, logit_grad, precision=PRECISE)
@@ -276,20 +297,27 @@
                 "cd,cf->df", ordered[:, low:high], hidden_rows, preferred_element_type=jnp.float32
             )
 
-        return scatter_sum(term_of, model_width)
-
-    down_term = jnp.stack(
-        [expert_term(slot_grad_ordered[at], active[at]).T for at in range(EXPERTS)]
-    )
-    up_term = jnp.stack(
-        [expert_term(dispatched_ordered[at], hidden_grad[at]) for at in range(EXPERTS)]
-    )
+        return ScatterSum(term_of, model_width)
+
+    groups = {
+        "down": [expert_term(slot_grad_ordered[at], active[at]) for at in range(EXPERTS)],
+        "up": [expert_term(dispatched_ordered[at], hidden_grad[at]) for at in range(EXPERTS)],
+    }
+    step_all(groups["down"])
+    step_all(groups["up"])
+    expert_done = second_grad[:8, :128]
+    step_all(groups["down"], expert_done)
+    if earlier:
+        step_all(earlier["heads"], expert_done)
+        step_all(earlier["up"], expert_done)
+        step_all(earlier["down"], expert_done)
     middle_grad, midnorm_term = jax.vjp(rms_norm, middle, midnorm_gain.astype(jnp.float32))[1](
         second_grad
     )
     middle_grad = upstream + middle_grad
     attn_grad = middle_grad.astype(jnp.bfloat16)
-    output_term = expert_term(jnp.dot(attn_grad, order), mixed_heads).T
+    output_sum = expert_term(jnp.dot(attn_grad, order), mixed_heads)
+    output_sum.step()
     mixed_grad = jnp.einsum(
         "td,fd->tf", attn_grad, output_weight, preferred_element_type=jnp.float32
     ).astype(jnp.bfloat16)
@@ -320,32 +348,50 @@
     query_back = query_back.reshape(row_count, -1).astype(jnp.bfloat16)
     key_back = key_back.reshape(row_count, -1).astype(jnp.bfloat16)
     value_back = value_back.reshape(row_count, -1).astype(jnp.bfloat16)
-    projection_term = expert_term(
+    projection_sum = expert_term(
         jnp.dot(normed, order), jnp.concatenate([query_back, key_back, value_back], axis=1)
     )
-    query_term, key_term, value_term = jnp.split(projection_term, 3, axis=1)
+    projection_sum.step()
+    groups["heads"] = [output_sum, projection_sum]
     normed_part = (
         jnp.einsum("tf,df->td", query_back, query_weight, preferred_element_type=jnp.float32)
         + jnp.einsum("tf,df->td", key_back, key_weight, preferred_element_type=jnp.float32)
         + jnp.einsum("tf,df->td", value_back, value_weight, preferred_element_type=jnp.float32)
     )
+    if earlier:
+        heads_done = normed_part[:8, :128]
+        step_all(groups["up"], heads_done)
+        step_all(earlier["heads"], heads_done)
+        step_all(earlier["up"], heads_done)
+        step_all(groups["down"], heads_done)
     normed_grad = exchange_sum(normed_part)
     stream_grad, prenorm_term = jax.vjp(rms_norm, stream, prenorm_gain.astype(jnp.float32))[1](
         normed_grad
     )
-    term_set = (
+    small_terms = (prenorm_term, midnorm_term, table_term, router_term)
+    return (middle_grad + stream_grad, groups, small_terms)
+
+
+def finished_terms(groups, small_terms):
+    for name in ("down", "up", "heads"):
+        for one in groups[name]:
+            while one.bit < one.size.bit_length() - 1:
+                one.step()
+    prenorm_term, midnorm_term, table_term, router_term = small_terms
+    output_sum, projection_sum = groups["heads"]
+    query_term, key_term, value_term = jnp.split(projection_sum.kept, 3, axis=1)
+    return (
         query_term,
         key_term,
         value_term,
-        output_term,
+        output_sum.kept.T,
         prenorm_term,
         midnorm_term,
         table_term,
         router_term,
-        up_term,
-        down_term,
-    )
-    return (middle_grad + stream_grad, term_set)
+        jnp.stack([one.kept for one in groups["up"]]),
+        jnp.stack([one.kept.T for one in groups["down"]]),
+    )
 
 
 def on_device(
@@ -401,10 +447,11 @@
         )
         saved_list.append(saved_state)
     upstream = cotangent.astype(jnp.float32) * alive_rows[:, None].astype(jnp.float32)
-    layer_terms = [None] * LAYERS
+    layer_sums = [None] * LAYERS
+    groups = None
     for layer_index in reversed(range(LAYERS)):
         weight_set = tuple((weight_arr[layer_index] for weight_arr in weight_all))
-        upstream, term_set = layer_backward_pass(
+        upstream, groups, small_terms = layer_backward_pass(
             upstream,
             saved_list[layer_index],
             weight_set,
@@ -413,8 +460,12 @@
             slot_indicator,
             bucket_indicator,
             order,
+            groups,
         )
-        layer_terms[layer_index] = term_set
+        layer_sums[layer_index] = (groups, small_terms)
+    layer_terms = [None] * LAYERS
+    for layer_index in reversed(range(LAYERS)):
+        layer_terms[layer_index] = finished_terms(*layer_sums[layer_index])
     (
         query_weight_grad,
         key_grad,

time: 980 us -> 909 us (0.928)
  waiting for transfers between devices: 574 us -> 521 us
  starting transfers between devices: 83 us -> 62.7 us
    ppermute x64, waiting for transfers between devices: 397 us -> 352 us  [step(): received = lax.ppermute(sent, 'dp', flip_pairs(self.size, self.bit))]
    ppermute x64, starting transfers between devices: 63.4 us -> 49.7 us  [step(): received = lax.ppermute(sent, 'dp', flip_pairs(self.size, self.bit))]
  transfers between devices with their start and end apart: 76 -> 76, of which waited for: 41 -> 40; matrix products, arithmetic and copies ran while one was open for 25% -> 27% of each run, Pallas kernels for 0% -> 0%
where the time goes in v2:
time: 909 us; the launch traced here: 905 us
  waiting for transfers between devices  521 us (57%)
  matrix products  238 us (26%)
  starting transfers between devices  62.7 us (7%)
  other arithmetic  54.9 us (6%)
  local copies, waits for them, and re-layouts  24.3 us (3%)
    ppermute x64, waiting for transfers between devices, step(): received = lax.ppermute(sent, 'dp', flip_pairs(self.size, self.bit))  352 us
    ppermute x8, waiting for transfers between devices, exchange_sum(): total = total + lax.ppermute(partial_value, 'tensor', pairs)  128 us
    dot_general x48, matrix products, term_of(): jnp.einsum('cd,cf->df', ordered[:, low:high], hidden_rows, preferred_elem...  99.1 us
    ppermute x64, starting transfers between devices, step(): received = lax.ppermute(sent, 'dp', flip_pairs(self.size, self.bit))  49.7 us
    ppermute x4, waiting for transfers between devices, doubling_sum(): values = values + lax.ppermute(values, 'dp', flip_pairs(size, bit))  41.1 us
  transfers between devices with their start and end apart: 76, of which 40 were waited for; matrix products, arithmetic and copies ran while one was open for 27% of the time, Pallas kernels for 0%

profile of v2, /device:TPU:0, one launch (start us, length us, event | category | flops | bytes accessed | tf_op | source)
XLA Modules:
  0.0 905.1 jit_solution(14689413279326789614)
XLA Ops:
  30.7 33.8 %collective-permute-done = f32[512,768]{1,0:T(8,128)S(1)} collective-permute-done((f32[512,768]{1,0:T(8,128)S(1)}, f32[512,768]{1,0:T(8,128)S(1)}, u32[]{:S(2)}, u32[]{:S(2)}) %collective-permute-start) | collective-permute-done | bytes 1572896 | tf_op jit(solution)/shard_map/ppermute | solution.py:60
  85.2 27.9 %collective-permute-done.1 = f32[512,768]{1,0:T(8,128)} collective-permute-done((f32[512,768]{1,0:T(8,128)}, f32[512,768]{1,0:T(8,128)}, u32[]{:S(2)}, u32[]{:S(2)}) %collective-permute-start.1) | collective-permute-done | bytes 1572896 | tf_op jit(solution)/shard_map/ppermute | solution.py:60
  135.7 27.1 %collective-permute-done.2 = f32[512,768]{1,0:T(8,128)S(1)} collective-permute-done((f32[512,768]{1,0:T(8,128)S(1)}, f32[512,768]{1,0:T(8,128)S(1)}, u32[]{:S(2)}, u32[]{:S(2)}) %collective-permute-start.2) | collective-permute-done | bytes 1572896 | tf_op jit(solution)/shard_map/ppermute | solution.py:60
  217.1 28.6 %collective-permute-done.4 = f32[512,768]{1,0:T(8,128)S(1)} collective-permute-done((f32[512,768]{1,0:T(8,128)S(1)}, f32[512,768]{1,0:T(8,128)S(1)}, u32[]{:S(2)}, u32[]{:S(2)}) %collective-permute-start.4) | collective-permute-done | bytes 1572896 | tf_op jit(solution)/shard_map/ppermute | solution.py:60
  386.3 10.3 %collective-permute-done.70 = f32[96,1536]{1,0:T(8,128)S(1)} collective-permute-done((f32[96,1536]{1,0:T(8,128)S(1)}, f32[96,1536]{1,0:T(8,128)S(1)}, u32[]{:S(2)}, u32[]{:S(2)}) %collective-permute-start.70) | collective-permute-done | bytes 589856 | tf_op jit(solution)/shard_map/ppermute | solution.py:94
  398.8 9.3 %collective-permute-done.66 = f32[96,1536]{1,0:T(8,128)S(1)} collective-permute-done((f32[96,1536]{1,0:T(8,128)S(1)}, f32[96,1536]{1,0:T(8,128)S(1)}, u32[]{:S(2)}, u32[]{:S(2)}) %collective-permute-start.66) | collective-permute-done | bytes 589856 | tf_op jit(solution)/shard_map/ppermute | solution.py:94
  410.7 19.8 %collective-permute-done.45 = f32[192,1536]{1,0:T(8,128)S(1)} collective-permute-done((f32[192,1536]{1,0:T(8,128)S(1)}, f32[192,1536]{1,0:T(8,128)S(1)}, u32[]{:S(2)}, u32[]{:S(2)}) %collective-permute-start.45) | collective-permute-done | bytes 1179680 | tf_op jit(solution)/shard_map/ppermute | solution.py:94
  431.6 23.5 %collective-permute-done.41 = f32[192,1536]{1,0:T(8,128)S(1)} collective-permute-done((f32[192,1536]{1,0:T(8,128)S(1)}, f32[192,1536]{1,0:T(8,128)S(1)}, u32[]{:S(2)}, u32[]{:S(2)}) %collective-permute-start.41) | collective-permute-done | bytes 1179680 | tf_op jit(solution)/shard_map/ppermute | solution.py:94
  503.5 15.8 %collective-permute-done.71 = f32[48,1536]{1,0:T(8,128)S(1)} collective-permute-done((f32[48,1536]{1,0:T(8,128)S(1)}, f32[48,1536]{1,0:T(8,128)S(1)}, u32[]{:S(2)}, u32[]{:S(2)}) %collective-permute-start.71) | collective-permute-done | bytes 294944 | tf_op jit(solution)/shard_map/ppermute | solution.py:94
  522.2 11.9 %collective-permute-done.67 = f32[48,1536]{1,0:T(8,128)S(1)} collective-permute-done((f32[48,1536]{1,0:T(8,128)S(1)}, f32[48,1536]{1,0:T(8,128)S(1)}, u32[]{:S(2)}, u32[]{:S(2)}) %collective-permute-start.67) | collective-permute-done | bytes 294944 | tf_op jit(solution)/shard_map/ppermute | solution.py:94
  534.2 9.7 %collective-permute-done.22 = f32[96,384]{1,0:T(8,128)S(1)} collective-permute-done((f32[96,384]{1,0:T(8,128)S(1)}, f32[96,384]{1,0:T(8,128)S(1)}, u32[]{:S(2)}, u32[]{:S(2)}) %collective-permute-start.22) | collective-permute-done | bytes 147488 | tf_op jit(solution)/shard_map/ppermute | solution.py:94
  551.4 14.1 %collective-permute-done.46 = f32[96,1536]{1,0:T(8,128)S(1)} collective-permute-done((f32[96,1536]{1,0:T(8,128)S(1)}, f32[96,1536]{1,0:T(8,128)S(1)}, u32[]{:S(2)}, u32[]{:S(2)}) %collective-permute-start.46) | collective-permute-done | bytes 589856 | tf_op jit(solution)/shard_map/ppermute | solution.py:94
  565.5 9.4 %collective-permute-done.42 = f32[96,1536]{1,0:T(8,128)S(1)} collective-permute-done((f32[96,1536]{1,0:T(8,128)S(1)}, f32[96,1536]{1,0:T(8,128)S(1)}, u32[]{:S(2)}, u32[]{:S(2)}) %collective-permute-start.42) | collective-permute-done | bytes 589856 | tf_op jit(solution)/shard_map/ppermute | solution.py:94
  610.4 17.6 %collective-permute-done.47 = f32[48,1536]{1,0:T(8,128)S(1)} collective-permute-done((f32[48,1536]{1,0:T(8,128)S(1)}, f32[48,1536]{1,0:T(8,128)S(1)}, u32[]{:S(2)}, u32[]{:S(2)}) %collective-permute-start.47) | collective-permute-done | bytes 294944 | tf_op jit(solution)/shard_map/ppermute | solution.py:94
  634.0 12.5 %collective-permute-done.18 = f32[96,384]{1,0:T(8,128)S(1)} collective-permute-done((f32[96,384]{1,0:T(8,128)S(1)}, f32[96,384]{1,0:T(8,128)S(1)}, u32[]{:S(2)}, u32[]{:S(2)}) %collective-permute-start.18) | collective-permute-done | bytes 147488 | tf_op jit(solution)/shard_map/ppermute | solution.py:94
  657.8 10.1 %collective-permute-done.15 = f32[48,1152]{1,0:T(8,128)S(1)} collective-permute-done((f32[48,1152]{1,0:T(8,128)}, f32[48,1152]{1,0:T(8,128)S(1)}, u32[]{:S(2)}, u32[]{:S(2)}) %collective-permute-start.15) | collective-permute-done | bytes 221216 | tf_op jit(solution)/shard_map/ppermute | solution.py:94
  671.4 35.8 %collective-permute-done.25 = f32[12,768]{1,0:T(8,128)S(1)} collective-permute-done((f32[12,768]{1,0:T(8,128)S(1)}, f32[12,768]{1,0:T(8,128)S(1)}, u32[]{:S(2)}, u32[]{:S(2)}) %collective-permute-start.25) | collective-permute-done | bytes 36896 | tf_op jit(solution)/shard_map/ppermute | solution.py:118
  732.4 13.2 %collective-permute-done.61 = f32[192,1536]{1,0:T(8,128)S(1)} collective-permute-done((f32[192,1536]{1,0:T(8,128)}, f32[192,1536]{1,0:T(8,128)S(1)}, u32[]{:S(2)}, u32[]{:S(2)}) %collective-permute-start.61) | collective-permute-done | bytes 1179680 | tf_op jit(solution)/shard_map/ppermute | solution.py:94
  746.7 24.2 %collective-permute-done.57 = f32[192,1536]{1,0:T(8,128)S(1)} collective-permute-done((f32[192,1536]{1,0:T(8,128)}, f32[192,1536]{1,0:T(8,128)S(1)}, u32[]{:S(2)}, u32[]{:S(2)}) %collective-permute-start.57) | collective-permute-done | bytes 1179680 | tf_op jit(solution)/shard_map/ppermute | solution.py:94
  771.9 24.2 %collective-permute-done.53 = f32[192,1536]{1,0:T(8,128)S(1)} collective-permute-done((f32[192,1536]{1,0:T(8,128)S(1)}, f32[192,1536]{1,0:T(8,128)S(1)}, u32[]{:S(2)}, u32[]{:S(2)}) %collective-permute-start.53) | collective-permute-done | bytes 1179680 | tf_op jit(solution)/shard_map/ppermute | solution.py:94
  801.3 17.6 %collective-permute-done.62 = f32[96,1536]{1,0:T(8,128)S(1)} collective-permute-done((f32[96,1536]{1,0:T(8,128)S(1)}, f32[96,1536]{1,0:T(8,128)S(1)}, u32[]{:S(2)}, u32[]{:S(2)}) %collective-permute-start.62) | collective-permute-done | bytes 589856 | tf_op jit(solution)/shard_map/ppermute | solution.py:94
  819.0 18.9 %collective-permute-done.58 = f32[96,1536]{1,0:T(8,128)S(1)} collective-permute-done((f32[96,1536]{1,0:T(8,128)S(1)}, f32[96,1536]{1,0:T(8,128)S(1)}, u32[]{:S(2)}, u32[]{:S(2)}) %collective-permute-start.58) | collective-permute-done | bytes 589856 | tf_op jit(solution)/shard_map/ppermute | solution.py:94
  851.8 23.4 %collective-permute-done.31 = f32[48,1536]{1,0:T(8,128)S(1)} collective-permute-done((f32[48,1536]{1,0:T(8,128)S(1)}, f32[48,1536]{1,0:T(8,128)S(1)}, u32[]{:S(2)}, u32[]{:S(2)}) %collective-permute-start.31) | collective-permute-done | bytes 294944 | tf_op jit(solution)/shard_map/ppermute | solution.py:94
  894.1 8.6 collective-permute-done.11
  (851 shorter events, 453.9 us)
Async XLA Ops:
  200.2 94.5 %collective-permute-start.48 = (f32[384,1536]{1,0:T(8,128)}, f32[384,1536]{1,0:T(8,128)}, u32[]{:S(2)}, u32[]{:S(2)}) collective-permute-start(f32[384,1536]{1,0:T(8,128)} %fusion.202), channel_id=1, source_target_pairs={{0,2},{2,0},{4,6},{6,4},{8,10},{10,8},{12,14},{14,12},{16,18},{18,... | collective-permute-start | bytes 7077896 | tf_op jit(solution)/shard_map/ppermute | solution.py:94
  202.1 98.2 %collective-permute-start.44 = (f32[384,1536]{1,0:T(8,128)}, f32[384,1536]{1,0:T(8,128)}, u32[]{:S(2)}, u32[]{:S(2)}) collective-permute-start(f32[384,1536]{1,0:T(8,128)} %fusion.199), channel_id=1, source_target_pairs={{0,2},{2,0},{4,6},{6,4},{8,10},{10,8},{12,14},{14,12},{16,18},{18,... | collective-permute-start | bytes 7077896 | tf_op jit(solution)/shard_map/ppermute | solution.py:94
  204.6 79.0 %collective-permute-start.72 = (f32[384,1536]{1,0:T(8,128)}, f32[384,1536]{1,0:T(8,128)}, u32[]{:S(2)}, u32[]{:S(2)}) collective-permute-start(f32[384,1536]{1,0:T(8,128)} %fusion.220), channel_id=1, source_target_pairs={{0,2},{2,0},{4,6},{6,4},{8,10},{10,8},{12,14},{14,12},{16,18},{18,... | collective-permute-start | bytes 7077896 | tf_op jit(solution)/shard_map/ppermute | solution.py:94
  215.6 75.5 %collective-permute-start.68 = (f32[384,1536]{1,0:T(8,128)}, f32[384,1536]{1,0:T(8,128)}, u32[]{:S(2)}, u32[]{:S(2)}) collective-permute-start(f32[384,1536]{1,0:T(8,128)} %fusion.217), channel_id=1, source_target_pairs={{0,2},{2,0},{4,6},{6,4},{8,10},{10,8},{12,14},{14,12},{16,18},{18,... | collective-permute-start | bytes 7077896 | tf_op jit(solution)/shard_map/ppermute | solution.py:94
  294.7 64.2 %collective-permute-start.12 = (f32[384,1152]{1,0:T(8,128)}, f32[384,1152]{1,0:T(8,128)}, u32[]{:S(2)}, u32[]{:S(2)}) collective-permute-start(f32[384,1152]{1,0:T(8,128)} %fusion.226), channel_id=1, source_target_pairs={{0,2},{2,0},{4,6},{6,4},{8,10},{10,8},{12,14},{14,12},{16,18},{18,... | collective-permute-start | bytes 5308424 | tf_op jit(solution)/shard_map/ppermute | solution.py:94
  300.3 66.2 %collective-permute-start.73 = (f32[192,1536]{1,0:T(8,128)}, f32[192,1536]{1,0:T(8,128)}, u32[]{:S(2)}, u32[]{:S(2)}) collective-permute-start(f32[192,1536]{1,0:T(8,128)} %slice_add_fusion), channel_id=1, source_target_pairs={{0,4},{2,6},{4,0},{6,2},{8,12},{10,14},{12,8},{14,10},{16,20},{18,... | collective-permute-start | bytes 3538952 | tf_op jit(solution)/shard_map/ppermute | solution.py:94
  307.1 61.4 %collective-permute-start.69 = (f32[192,1536]{1,0:T(8,128)}, f32[192,1536]{1,0:T(8,128)}, u32[]{:S(2)}, u32[]{:S(2)}) collective-permute-start(f32[192,1536]{1,0:T(8,128)} %slice_add_fusion.2), channel_id=1, source_target_pairs={{0,4},{2,6},{4,0},{6,2},{8,12},{10,14},{12,8},{14,10},{16,20},{18,... | collective-permute-start | bytes 3538952 | tf_op jit(solution)/shard_map/ppermute | solution.py:94
  310.4 69.6 %collective-permute-start.65 = (f32[192,1536]{1,0:T(8,128)}, f32[192,1536]{1,0:T(8,128)}, u32[]{:S(2)}, u32[]{:S(2)}) collective-permute-start(f32[192,1536]{1,0:T(8,128)} %slice_add_fusion.4), channel_id=1, source_target_pairs={{0,4},{2,6},{4,0},{6,2},{8,12},{10,14},{12,8},{14,10},{16,20},{18,... | collective-permute-start | bytes 3538952 | tf_op jit(solution)/shard_map/ppermute | solution.py:94
  343.4 112.9 %collective-permute-start.6 = (f32[512,768]{1,0:T(8,128)S(1)}, f32[512,768]{1,0:T(8,128)}, u32[]{:S(2)}, u32[]{:S(2)}) collective-permute-start(f32[512,768]{1,0:T(8,128)S(1)} %convolution_add_fusion), channel_id=1, source_target_pairs={{0,1},{1,0},{2,3},{3,2},{4,5},{5,4},{6,7},{7,6},{8,9},{9,8},{10,11... | collective-permute-start | bytes 4718600 | tf_op jit(solution)/shard_map/ppermute | solution.py:60
  366.5 63.9 %collective-permute-start.45 = (f32[192,1536]{1,0:T(8,128)S(1)}, f32[192,1536]{1,0:T(8,128)S(1)}, u32[]{:S(2)}, u32[]{:S(2)}) collective-permute-start(f32[192,1536]{1,0:T(8,128)S(1)} %copy-done.126), channel_id=1, source_target_pairs={{0,4},{2,6},{4,0},{6,2},{8,12},{10,14},{12,8},{14,10},{16,20},{18,... | collective-permute-start | bytes 3538952 | tf_op jit(solution)/shard_map/ppermute | solution.py:94
  396.6 58.6 %collective-permute-start.41 = (f32[192,1536]{1,0:T(8,128)S(1)}, f32[192,1536]{1,0:T(8,128)S(1)}, u32[]{:S(2)}, u32[]{:S(2)}) collective-permute-start(f32[192,1536]{1,0:T(8,128)S(1)} %copy-done.127), channel_id=1, source_target_pairs={{0,4},{2,6},{4,0},{6,2},{8,12},{10,14},{12,8},{14,10},{16,20},{18,... | collective-permute-start | bytes 3538952 | tf_op jit(solution)/shard_map/ppermute | solution.py:94
  408.1 166.9 %collective-permute-start.36 = (f32[384,1536]{1,0:T(8,128)}, f32[384,1536]{1,0:T(8,128)}, u32[]{:S(2)}, u32[]{:S(2)}) collective-permute-start(f32[384,1536]{1,0:T(8,128)} %fusion.193), channel_id=1, source_target_pairs={{0,2},{2,0},{4,6},{6,4},{8,10},{10,8},{12,14},{14,12},{16,18},{18,... | collective-permute-start | bytes 7077896 | tf_op jit(solution)/shard_map/ppermute | solution.py:94
  409.0 172.3 %collective-permute-start.32 = (f32[384,1536]{1,0:T(8,128)}, f32[384,1536]{1,0:T(8,128)}, u32[]{:S(2)}, u32[]{:S(2)}) collective-permute-start(f32[384,1536]{1,0:T(8,128)} %fusion.190), channel_id=1, source_target_pairs={{0,2},{2,0},{4,6},{6,4},{8,10},{10,8},{12,14},{14,12},{16,18},{18,... | collective-permute-start | bytes 7077896 | tf_op jit(solution)/shard_map/ppermute | solution.py:94
  485.9 63.3 %collective-permute-start.16 = (f32[384,384]{1,0:T(8,128)}, f32[384,384]{1,0:T(8,128)}, u32[]{:S(2)}, u32[]{:S(2)}) collective-permute-start(f32[384,384]{1,0:T(8,128)} %fusion.224), channel_id=1, source_target_pairs={{0,2},{2,0},{4,6},{6,4},{8,10},{10,8},{12,14},{14,12},{16,18},{18,... | collective-permute-start | bytes 1769480 | tf_op jit(solution)/shard_map/ppermute | solution.py:94
  581.3 74.9 %collective-permute-start.7 = (f32[512,768]{1,0:T(8,128)S(1)}, f32[512,768]{1,0:T(8,128)S(1)}, u32[]{:S(2)}, u32[]{:S(2)}) collective-permute-start(f32[512,768]{1,0:T(8,128)S(1)} %add_add_fusion.4), channel_id=1, source_target_pairs={{0,1},{1,0},{2,3},{3,2},{4,5},{5,4},{6,7},{7,6},{8,9},{9,8},{10,11... | collective-permute-start | bytes 4718600 | tf_op jit(solution)/shard_map/ppermute | solution.py:60
  587.7 132.4 %collective-permute-start.8 = (f32[384,1152]{1,0:T(8,128)}, f32[384,1152]{1,0:T(8,128)}, u32[]{:S(2)}, u32[]{:S(2)}) collective-permute-start(f32[384,1152]{1,0:T(8,128)} %fusion.228), channel_id=1, source_target_pairs={{0,2},{2,0},{4,6},{6,4},{8,10},{10,8},{12,14},{14,12},{16,18},{18,... | collective-permute-start | bytes 5308424 | tf_op jit(solution)/shard_map/ppermute | solution.py:94
  628.0 96.9 %collective-permute-start.37 = (f32[192,1536]{1,0:T(8,128)}, f32[192,1536]{1,0:T(8,128)}, u32[]{:S(2)}, u32[]{:S(2)}) collective-permute-start(f32[192,1536]{1,0:T(8,128)} %slice_add_fusion.18), channel_id=1, source_target_pairs={{0,4},{2,6},{4,0},{6,2},{8,12},{10,14},{12,8},{14,10},{16,20},{18,... | collective-permute-start | bytes 3538952 | tf_op jit(solution)/shard_map/ppermute | solution.py:94
  652.8 75.2 %collective-permute-start.33 = (f32[192,1536]{1,0:T(8,128)}, f32[192,1536]{1,0:T(8,128)}, u32[]{:S(2)}, u32[]{:S(2)}) collective-permute-start(f32[192,1536]{1,0:T(8,128)} %slice_add_fusion.20), channel_id=1, source_target_pairs={{0,4},{2,6},{4,0},{6,2},{8,12},{10,14},{12,8},{14,10},{16,20},{18,... | collective-permute-start | bytes 3538952 | tf_op jit(solution)/shard_map/ppermute | solution.py:94
  655.0 75.0 %collective-permute-start.29 = (f32[192,1536]{1,0:T(8,128)}, f32[192,1536]{1,0:T(8,128)}, u32[]{:S(2)}, u32[]{:S(2)}) collective-permute-start(f32[192,1536]{1,0:T(8,128)} %slice_add_fusion.22), channel_id=1, source_target_pairs={{0,4},{2,6},{4,0},{6,2},{8,12},{10,14},{12,8},{14,10},{16,20},{18,... | collective-permute-start | bytes 3538952 | tf_op jit(solution)/shard_map/ppermute | solution.py:94
  720.1 50.8 %collective-permute-start.57 = (f32[192,1536]{1,0:T(8,128)}, f32[192,1536]{1,0:T(8,128)S(1)}, u32[]{:S(2)}, u32[]{:S(2)}) collective-permute-start(f32[192,1536]{1,0:T(8,128)} %slice_add_fusion.8), channel_id=1, source_target_pairs={{0,4},{2,6},{4,0},{6,2},{8,12},{10,14},{12,8},{14,10},{16,20},{18,... | collective-permute-start | bytes 3538952 | tf_op jit(solution)/shard_map/ppermute | solution.py:94
  724.9 71.2 %collective-permute-start.53 = (f32[192,1536]{1,0:T(8,128)S(1)}, f32[192,1536]{1,0:T(8,128)S(1)}, u32[]{:S(2)}, u32[]{:S(2)}) collective-permute-start(f32[192,1536]{1,0:T(8,128)S(1)} %copy-done.125), channel_id=1, source_target_pairs={{0,4},{2,6},{4,0},{6,2},{8,12},{10,14},{12,8},{14,10},{16,20},{18,... | collective-permute-start | bytes 3538952 | tf_op jit(solution)/shard_map/ppermute | solution.py:94
  728.0 118.3 %collective-permute-start.9 = (f32[192,1152]{1,0:T(8,128)S(1)}, f32[192,1152]{1,0:T(8,128)S(1)}, u32[]{:S(2)}, u32[]{:S(2)}) collective-permute-start(f32[192,1152]{1,0:T(8,128)S(1)} %slice_add_fusion.26), channel_id=1, source_target_pairs={{0,4},{2,6},{4,0},{6,2},{8,12},{10,14},{12,8},{14,10},{16,20},{18,... | collective-permute-start | bytes 2654216 | tf_op jit(solution)/shard_map/ppermute | solution.py:94
  730.0 67.2 %collective-permute-start.38 = (f32[96,1536]{1,0:T(8,128)S(1)}, f32[96,1536]{1,0:T(8,128)S(1)}, u32[]{:S(2)}, u32[]{:S(2)}) collective-permute-start(f32[96,1536]{1,0:T(8,128)S(1)} %get-tuple-element.142), channel_id=1, source_target_pairs={{0,8},{2,10},{4,12},{6,14},{8,0},{10,2},{12,4},{14,6},{16,24},{18,... | collective-permute-start | bytes 1769480 | tf_op jit(solution)/shard_map/ppermute | solution.py:94
  745.6 52.8 %collective-permute-start.34 = (f32[96,1536]{1,0:T(8,128)S(1)}, f32[96,1536]{1,0:T(8,128)S(1)}, u32[]{:S(2)}, u32[]{:S(2)}) collective-permute-start(f32[96,1536]{1,0:T(8,128)S(1)} %get-tuple-element.140), channel_id=1, source_target_pairs={{0,8},{2,10},{4,12},{6,14},{8,0},{10,2},{12,4},{14,6},{16,24},{18,... | collective-permute-start | bytes 1769480 | tf_op jit(solution)/shard_map/ppermute | solution.py:94
  (283 other events, 4417.1 us)
